TPU v7x, 128 devices: a whole 4x4x4 slice. The times are simulated.
128 devices in a mesh: tm: 32 (over z, y, core), space: 4 (over x).
Axes of the slice: x: 4, y: 4, z: 4, core: 2. Of those that a mesh axis runs over, the one named last changes fastest.
Arguments:
- tokens: bfloat16 [65536, 2240], P('tm'), may hold values from -6 to 6
- mod_scale: float32 [2240], replicated, may hold values from -1.5 to 1.5
- mod_shift: float32 [2240], replicated, may hold values from -3 to 3
- out_gate: float32 [2240], replicated, may hold values from -4 to 4
- w_query: bfloat16 [2240, 2240], P(None, 'space'), may hold values from -0.125 to 0.125
- w_key: bfloat16 [2240, 2240], P(None, 'space'), may hold values from -0.125 to 0.125
- w_value: bfloat16 [2240, 2240], P(None, 'space'), may hold values from -0.125 to 0.125
- w_out: bfloat16 [2240, 2240], P('space'), may hold values from -0.125 to 0.125
- log_decay: float32 [128, 20], P('tm', 'space'), may hold values from -8 to 0
- mix_weight: bfloat16 [8, 16, 16], replicated, may hold values from -0.5 to 0.5
- block_last: int32 [128], P('tm'), may hold values from 0 to 127, as said below
- win_list: int32 [128, 32, 8], replicated, may hold values from 0 to 127, as said below
Outputs:
- out: bfloat16 [65536, 2240], P(('tm', 'space'))
Inputs may be any that keep to these rules, and one draw needn't show every extreme that they name: `block_last`: frame blocks are runs of consecutive frames that never cross a boundary between the groups of 4 frames that start at multiples of 4; each entry is at least its own frame's index and at most the last frame of that group. `win_list`: every listed frame lies within 2 frames of the frame that lists it; slot 0 names the frame 2 earlier and slot 1 the frame 2 later, each clipped to 0 .. 127.
All inputs are finite; a program needn't handle non-finite values.
Results may differ from a plain program's by a relative error of at most 0.015.
Values may be sent and summed in bfloat16 or wider, within the bound.
A program may use at most 192 MiB of HBM per device.

v0:
```python
import jax
import jax.numpy as jnp
from jax import lax
from jax.sharding import PartitionSpec as P

HEAD_DIM = 112
TILES = 32
TT = 16
WIN = 2


epsilon = 1e-06
highest = lax.Precision.HIGHEST


def entering(array, axis, join, neutral):
    place = lax.axis_index(axis)
    gathered = jax.tree.map(
        lambda a, kind: lax.all_gather(a.astype(kind), axis), array, (jnp.bfloat16, jnp.bfloat16)
    )
    state = jax.tree.map(lambda a, e: jnp.zeros_like(a) + jnp.asarray(e, a.dtype), array, neutral)

    def one(lap, state):
        return join(
            state,
            jax.tree.map(
                lambda a, own: lax.dynamic_index_in_dim(a, lap, 0, False).astype(own.dtype),
                gathered,
                array,
            ),
        )

    return lax.fori_loop(0, place, one, state)


def unit_rms(values):
    return values * lax.rsqrt(jnp.mean(values * values, axis=-1, keepdims=True) + epsilon)


def mix_tiles(padded, offsets, mix_weight):
    frames = offsets.shape[0]
    shifts = jnp.arange(-WIN, WIN + 1, dtype=jnp.int32)
    select = (offsets[..., None] == shifts).astype(jnp.float32)
    matrices = jnp.einsum(
        "fjns,npq->sfjpq", select, mix_weight.astype(jnp.float32), precision=highest
    )
    blended = jnp.zeros((frames,) + padded.shape[1:], jnp.float32)
    for shift_index in range(2 * WIN + 1):
        sliced = padded[shift_index : shift_index + frames].astype(jnp.float32)
        blended = blended + jnp.einsum(
            "fjpq,fjqc->fjpc", matrices[shift_index], sliced, precision=highest
        )
    return blended.astype(jnp.bfloat16)


def fold_states(earlier_part, later_part):
    return (
        earlier_part[0] + later_part[0],
        jnp.exp(later_part[0])[:, None, None] * earlier_part[1] + later_part[1],
    )


def round_term(product):
    return lax.optimization_barrier(product.astype(jnp.bfloat16)).astype(jnp.float32)


def body(
    tokens,
    mod_scale,
    mod_shift,
    out_gate,
    w_query,
    w_key,
    w_value,
    w_out,
    log_decay,
    mix_weight,
    block_last,
    win_list,
):
    tok_rows, model_width = tokens.shape
    head_cols = w_query.shape[1]
    local_heads = head_cols // HEAD_DIM
    frame_count = log_decay.shape[0]
    frame_rows = tok_rows // frame_count
    normed = (unit_rms(tokens.astype(jnp.float32)) * (1.0 + mod_scale) + mod_shift).astype(
        jnp.bfloat16
    )
    queries = jnp.dot(normed, w_query, preferred_element_type=jnp.float32).astype(jnp.bfloat16)
    key_proj = jnp.dot(normed, w_key, preferred_element_type=jnp.float32).astype(jnp.bfloat16)
    values = jnp.dot(normed, w_value, preferred_element_type=jnp.float32).astype(jnp.bfloat16)
    head_shape = (frame_count, frame_rows, local_heads, HEAD_DIM)
    kv_frames = jnp.einsum(
        "fthd,fthe->fhde",
        key_proj.reshape(head_shape),
        values.reshape(head_shape),
        preferred_element_type=jnp.float32,
    )

    def advance(running_state, inputs):
        decay_log, fresh_kv = inputs
        running_state = jnp.exp(decay_log)[:, None, None] * running_state + fresh_kv
        return (running_state, running_state)

    zero_state = jnp.zeros((local_heads, HEAD_DIM, HEAD_DIM), jnp.float32)
    zero_log = jnp.zeros((local_heads,), jnp.float32)
    last_state, local_states = lax.scan(advance, zero_state, (log_decay, kv_frames))
    total_log = jnp.sum(log_decay, axis=0)
    tm_index = lax.axis_index("tm")
    incoming = entering((total_log, last_state), "tm", fold_states, (zero_log, zero_state))[1]
    cum_log = jnp.cumsum(log_decay, axis=0)
    full_states = local_states + jnp.exp(cum_log)[:, :, None, None] * incoming[None]
    local_last = block_last - tm_index * frame_count
    picker = (local_last[:, None] == jnp.arange(frame_count, dtype=jnp.int32)[None, :]).astype(
        jnp.float32
    )
    read_states = jnp.einsum("fg,ghde->fhde", picker, full_states, precision=highest)
    linear = jnp.einsum(
        "fthd,fhde->fthe",
        queries.reshape(head_shape).astype(jnp.float32),
        read_states,
        precision=highest,
    )
    linear = unit_rms(linear).reshape(tok_rows, head_cols)
    value_tiles = values.reshape(frame_count, TILES, TT, head_cols)
    spatial = lax.all_to_all(value_tiles, "tm", split_axis=1, concat_axis=0, tiled=True)
    tiles_here = spatial.shape[1]
    all_frames = spatial.shape[0]
    frame_lists = lax.dynamic_slice_in_dim(win_list, tm_index * tiles_here, tiles_here, 1)
    relative = frame_lists - jnp.arange(all_frames, dtype=jnp.int32)[:, None, None]
    widened = jnp.pad(spatial, ((WIN, WIN), (0, 0), (0, 0), (0, 0)))
    blended = mix_tiles(widened, relative, mix_weight)
    window = lax.all_to_all(blended, "tm", split_axis=0, concat_axis=1, tiled=True)
    mixed_heads = (linear + window.reshape(tok_rows, head_cols).astype(jnp.float32)).astype(
        jnp.bfloat16
    )
    share_rows = tok_rows // lax.axis_size("space")
    summed = lax.psum_scatter(
        round_term(jnp.dot(mixed_heads, w_out, preferred_element_type=jnp.float32)).astype(
            jnp.bfloat16
        ),
        "space",
        scatter_dimension=0,
        tiled=True,
    ).astype(jnp.float32)
    own_tokens = lax.dynamic_slice_in_dim(
        tokens, lax.axis_index("space") * share_rows, share_rows, 0
    ).astype(jnp.float32)
    return (own_tokens + out_gate * summed).astype(jnp.bfloat16)


def solution(mesh):
    placed = (
        P("tm", None),
        P(),
        P(),
        P(),
        P(None, "space"),
        P(None, "space"),
        P(None, "space"),
        P("space", None),
        P("tm", "space"),
        P(),
        P("tm"),
        P(),
    )
    return jax.shard_map(
        body, mesh=mesh, in_specs=placed, out_specs=P(("tm", "space"), None), check_vma=False
    )
```

profile of v0, /device:TPU:0, one launch (start us, length us, event | category | flops | bytes accessed | tf_op | source)
XLA Modules:
  0.0 416.8 jit_solution(8054081729616778444)
XLA Ops:
  6.5 0.0 all-gather.4.cloned.1.call-start
  6.5 0.0 copy-start.7
  6.6 5.6 %fusion.2 = f32[2048]{0:T(1024)S(1)} fusion(bf16[2048,2240]{0,1:T(8,128)(2,1)} %param.16), kind=kLoop, calls=%fused_computation.10 | loop fusion | flops 13760512 | bytes 9183232 | tf_op jit(solution)/shard_map/reduce_sum | solution.py:37
  12.2 9.9 %fusion.5 = bf16[2048,2240]{0,1:T(8,128)(2,1)} fusion(bf16[2048,2240]{0,1:T(8,128)(2,1)} %param.16, f32[2240]{0:T(1024)S(1)} %copy-done.7, f32[2240]{0:T(1024)S(1)} %broadcast_add_fusion, f32[2048]{0:T(1024)S(1)} %add_rsqrt_fusion.1), kind=kLoop, calls=%fused_computation.13 | loop fusion | flops 22937600 | bytes 18376192 | tf_op jit(solution)/shard_map/convert_element_type | solution.py:86
  22.1 10.3 %convolution_convert_fusion.2 = bf16[2048,560]{0,1:T(8,128)(2,1)} fusion(bf16[2240,560]{0,1:T(8,128)(2,1)} %param.22, bf16[2048,2240]{0,1:T(8,128)(2,1)} %fusion.5), kind=kOutput, calls=%fused_computation.22 | convolution fusion | flops 5139169280 | bytes 13977600 | tf_op jit(solution)/shard_map/dot_general | solution.py:91
  32.4 6.0 %reshape.133 = bf16[4,512,5,112]{1,0,3,2:T(4,128)(2,1)} reshape(bf16[2048,560]{0,1:T(8,128)(2,1)} %convolution_convert_fusion.2) | data formatting | bytes 4587520 | tf_op jit(solution)/shard_map/reshape | solution.py:96
  38.4 9.9 %convolution_convert_fusion.3 = bf16[2048,560]{0,1:T(8,128)(2,1)} fusion(bf16[2240,560]{0,1:T(8,128)(2,1)} %param.21, bf16[2048,2240]{0,1:T(8,128)(2,1)} %fusion.5), kind=kOutput, calls=%fused_computation.23 | convolution fusion | flops 5139169280 | bytes 13977600 | tf_op jit(solution)/shard_map/dot_general | solution.py:90
  48.3 6.0 %reshape.132 = bf16[4,512,5,112]{1,0,3,2:T(4,128)(2,1)} reshape(bf16[2048,560]{0,1:T(8,128)(2,1)} %convolution_convert_fusion.3) | data formatting | bytes 4587520 | tf_op jit(solution)/shard_map/reshape | solution.py:95
  54.2 4.7 %fusion.24 = f32[4,5,112,112]{3,2,1,0:T(8,128)} fusion(bf16[4,512,5,112]{1,0,3,2:T(4,128)(2,1)} %reshape.133, bf16[4,512,5,112]{1,0,3,2:T(4,128)(2,1)} %reshape.132), kind=kOutput, calls=%fused_computation.39 | convolution fusion | flops 256901120 | bytes 5591040 | tf_op jit(solution)/shard_map/fthd,fthe->fhde/dot_general | solution.py:93
  59.0 7.2 %while.26 = (s32[]{:T(128)}, f32[5,112,112]{2,1,0:T(8,128)S(1)}, f32[4,5,112,112]{3,2,1,0:T(8,128)}, f32[4,5]{1,0:T(4,128)S(1)}, f32[4,5,112,112]{3,2,1,0:T(8,128)}, /*index=5*/s32[]{:T(128)}, s32[]{:T(128)}) while((s32[]{:T(128)}, f32[5,112,112]{2,1,0:T(8,128)S(1)}, f32[4,5,112,112]{3,2,1,0:T(8,128)}, f32[4,5]{1,0:T(4,128)S(1)}, ...), condition=%wide.region_2.3_spmd.clone, body=%wide.region_1.2_spmd.clone.sunk | while | flops 188163 | bytes 1075363 | solution.py:107
  59.0 1.8 bitcast_dynamic-update-slice_fusion.2
  60.7 1.8 bitcast_dynamic-update-slice_fusion.2
  62.5 1.8 bitcast_dynamic-update-slice_fusion.2
  64.4 1.8 bitcast_dynamic-update-slice_fusion.2
  66.2 0.7 convert_element_type.100
  66.9 0.0 all-gather.4.cloned.1.call-update
  66.9 4.3 %copy.46 = bf16[2048,560]{1,0:T(8,128)(2,1)} copy(bf16[2048,560]{0,1:T(8,128)(2,1)} %convolution_convert_fusion.2) | data formatting | bytes 4587520 | tf_op jit(solution)/shard_map/convert_element_type | solution.py:91
  71.2 3.7 copy.47
  74.9 8.8 %all-to-all-start = ((bf16[4,32,16,560]{3,2,0,1:T(8,128)(2,1)}), bf16[4,32,16,560]{3,2,0,1:T(8,128)(2,1)}, u32[]{:S(2)}, u32[]{:S(2)}) async-start(bf16[4,32,16,560]{3,2,0,1:T(8,128)(2,1)} %copy.47), calls=%async_computation | async-start | bytes 5242880 | tf_op jit(solution)/shard_map/all_to_all | solution.py:126
  83.7 0.7 subtract_bitcast_fusion
  84.4 0.3 convolution_bitcast_fusion
  84.8 1.4 copy.48
  86.2 1.4 copy.52
  87.6 1.4 copy.51
  89.0 1.4 copy.50
  90.4 1.4 copy.49
  91.8 28.4 %all-to-all-done = bf16[4,32,16,560]{3,2,0,1:T(8,128)(2,1)} async-done(((bf16[4,32,16,560]{3,2,0,1:T(8,128)(2,1)}), bf16[4,32,16,560]{3,2,0,1:T(8,128)(2,1)}, u32[]{:S(2)}, u32[]{:S(2)}) %all-to-all-start) | async-done | bytes 2293792 | tf_op jit(solution)/shard_map/all_to_all | solution.py:126
  120.2 4.4 %fusion.12 = f32[128,16,560]{2,1,0:T(8,128)S(1)} fusion(f32[128,16,16]{2,1,0:T(8,128)} %copy.49, bf16[128,1,16,560]{3,2,0,1:T(8,128)(2,1)} %bitcast.18), kind=kOutput, calls=%fused_computation.29 | convolution fusion | flops 220200960 | bytes 7012352 | tf_op jit(solution)/shard_map/fjpq,fjqc->fjpc/dot_general | solution.py:50
  124.6 0.0 copy-done.4
  124.6 0.0 copy-start.2
  124.6 4.0 fusion.10
  128.7 0.0 copy-done.2
  128.7 0.0 copy-start.3
  128.7 4.0 fusion.8
  132.7 6.4 %fusion.47 = f32[128,16,560]{2,1,0:T(8,128)} fusion(f32[128,16,16]{2,1,0:T(8,128)S(1)} %copy-done.3, bf16[128,16,560]{2,1,0:T(8,128)(2,1)} %bitcast.26), kind=kOutput, calls=%fused_computation.75 | convolution fusion | flops 220200960 | bytes 7012352 | tf_op jit(solution)/shard_map/fjpq,fjqc->fjpc/dot_general | solution.py:50
  139.2 0.0 copy-done.5
  139.2 8.2 %fusion.7 = bf16[128,1,16,560]{3,2,1,0:T(8,128)(2,1)} fusion(f32[128,16,560]{2,1,0:T(8,128)S(1)} %fusion.8, f32[128,16,560]{2,1,0:T(8,128)S(1)} %fusion.10, f32[128,16,560]{2,1,0:T(8,128)} %fusion.47, f32[128,16,560]{2,1,0:T(8,128)S(1)} %fusion.12, f32[128,16,16]{2,1,0:T(8,128)S(1)} %copy-done.5, bf16[128,1,16,560]{3,2,0,1:T(8,128)(2,1)} %bitcast.18), kind=kOutput, calls=%fused_computation.24 | convolution fusion | flops 225935360 | bytes 23068672 | tf_op jit(solution)/shard_map/fjpq,fjqc->fjpc/dot_general | solution.py:50
  147.4 4.9 %all-to-all-start.1 = ((bf16[128,1,16,560]{3,2,1,0:T(8,128)(2,1)}), bf16[128,1,16,560]{3,2,1,0:T(8,128)(2,1)}, u32[]{:S(2)}, u32[]{:S(2)}) async-start(bf16[128,1,16,560]{3,2,1,0:T(8,128)(2,1)} %fusion.7), calls=%async_computation.1 | async-start | bytes 5242880 | tf_op jit(solution)/shard_map/all_to_all | solution.py:133
  152.3 0.0 reduce-scatter.2.cloned.1.call-start
  152.4 0.6 dynamic-slice
  153.7 0.2 dynamic-update-slice
  153.9 87.5 %all-reduce.1 = bf16[160]{0:T(256)(128)(2,1)S(1)} all-reduce(bf16[160]{0:T(256)(128)(2,1)S(1)} %dynamic-update-slice), channel_id=2, replica_groups=mesh['tm'=32,'space'=4] {'tm'}, use_global_device_ids=true, to_apply=%add.1 | all-reduce | flops 160 | bytes 640
  241.4 0.1 reshape.150
  241.5 9.8 %convolution_convert_fusion.1 = bf16[2048,560]{0,1:T(8,128)(2,1)} fusion(bf16[2240,560]{0,1:T(8,128)(2,1)} %param.20, bf16[2048,2240]{0,1:T(8,128)(2,1)} %fusion.5), kind=kOutput, calls=%fused_computation.21 | convolution fusion | flops 5139169280 | bytes 13977600 | tf_op jit(solution)/shard_map/dot_general | solution.py:89
  251.4 6.0 %reshape.134 = bf16[4,512,5,112]{1,0,3,2:T(4,128)(2,1)} reshape(bf16[2048,560]{0,1:T(8,128)(2,1)} %convolution_convert_fusion.1) | data formatting | bytes 4587520 | tf_op jit(solution)/shard_map/reshape | solution.py:120
  257.4 0.0 all-to-all-done.1
  257.4 4.5 %copy.54 = f32[32,4,1,16,560]{4,3,0,1,2:T(8,128)} copy(bf16[32,4,1,16,560]{4,3,1,0,2:T(8,128)(2,1)} %bitcast.45) | data formatting | bytes 6881280 | tf_op jit(solution)/shard_map/convert_element_type | solution.py:134
  261.9 5.8 %copy.55 = f32[2048,560]{0,1:T(8,128)} copy(f32[2048,560]{1,0:T(8,128)} %bitcast.113) | data formatting | bytes 9175040 | tf_op jit(solution)/shard_map/convert_element_type | solution.py:134
  267.7 0.3 while.25
  268.0 1.6 multiply_add_fusion
  269.5 1.4 fusion.32
  271.0 0.0 copy-done.1
  271.0 2.6 fusion.6
  273.6 0.6 bitcast_multiply_fusion
  274.2 0.0 slice-start
  274.2 3.0 copy.44
  277.2 0.0 slice-start.1
  277.2 2.2 copy.58
  279.4 0.0 copy-done
  279.4 0.0 slice-done
  279.5 10.1 %convolution_convert_fusion = bf16[2048,2240]{0,1:T(8,128)(2,1)} fusion(bf16[560,2240]{1,0:T(8,128)(2,1)S(1)} %copy-done, f32[2048,560]{0,1:T(8,128)S(1)} %bitcast.118, f32[2048,560]{0,1:T(8,128)S(1)} %bitcast.117), kind=kOutput, calls=%fused_computation.14 | convolution fusion | flops 5144903680 | bytes 20858880 | tf_op jit(solution)/shard_map/dot_general | solution.py:139
  289.5 0.0 reduce-scatter.2.cloned.1.call-update
  289.6 115.4 %reduce-scatter.2.cloned.1.call-done = bf16[512,2240]{0,1:T(8,128)(2,1)} async-done(((bf16[2048,2240]{0,1:T(8,128)(2,1)}), bf16[512,2240]{0,1:T(8,128)(2,1)}) %reduce-scatter.2.cloned.1.call-update) | async-done | bytes 2293776 | tf_op jit(solution)/shard_map/reduce_scatter | solution.py:138
  405.0 4.5 %add_convert_fusion.1 = bf16[512,2240]{0,1:T(8,128)(2,1)} fusion(bf16[512,2240]{0,1:T(8,128)(2,1)} %reduce-scatter.2.cloned.1.call-done, f32[2240]{0:T(1024)S(1)} %copy-done.8, bf16[2048,2240]{0,1:T(8,128)(2,1)} %param.16, s32[]{:T(128)S(6)} %select_n.13), kind=kLoop, calls=%fused_computation.19 | loop fusion | flops 5734400 | bytes 6890244 | tf_op jit(solution)/shard_map/convert_element_type | solution.py:149
  (38 shorter events, 0.2 us)
Async XLA Ops:
  6.5 272.9 %copy-start = (bf16[560,2240]{1,0:T(8,128)(2,1)S(1)}, bf16[560,2240]{1,0:T(8,128)(2,1)}, u32[]{:S(2)}) copy-start(bf16[560,2240]{1,0:T(8,128)(2,1)} %param.23) | copy-start | bytes 7526404
  6.5 261.1 %all-gather.4.cloned.1.call-start = ((), (), s32[]{:S(2)}) async-start(), calls=%async_computation.4 | async-start | bytes 4730880 | tf_op jit(solution)/shard_map/all_gather | solution.py:19
  6.5 5.7 %copy-start.9 = (f32[2240]{0:T(1024)S(1)}, f32[2240]{0:T(1024)}, u32[]{:S(2)}) copy-start(f32[2240]{0:T(1024)} %param.17) | copy-start | bytes 26884
  6.5 5.7 %copy-start.7 = (f32[2240]{0:T(1024)S(1)}, f32[2240]{0:T(1024)}, u32[]{:S(2)}) copy-start(f32[2240]{0:T(1024)} %param.18) | copy-start | bytes 26884
  54.2 4.7 %copy-start.10 = (f32[4,5]{1,0:T(4,128)S(1)}, f32[4,5]{1,0:T(4,128)}, u32[]{:S(2)}) copy-start(f32[4,5]{1,0:T(4,128)} %param.24) | copy-start | bytes 244
  74.9 9.6 %copy-start.6 = (bf16[8,16,16]{2,1,0:T(8,128)(2,1)S(1)}, bf16[8,16,16]{2,1,0:T(8,128)(2,1)}, u32[]{:S(2)}) copy-start(bf16[8,16,16]{2,1,0:T(8,128)(2,1)} %param.25) | copy-start | bytes 12292
  74.9 45.3 %all-to-all-start = ((bf16[4,32,16,560]{3,2,0,1:T(8,128)(2,1)}), bf16[4,32,16,560]{3,2,0,1:T(8,128)(2,1)}, u32[]{:S(2)}, u32[]{:S(2)}) async-start(bf16[4,32,16,560]{3,2,0,1:T(8,128)(2,1)} %copy.47), calls=%async_computation | async-start | bytes 5242880 | tf_op jit(solution)/shard_map/all_to_all | solution.py:126
  120.2 4.4 %copy-start.4 = (f32[128,16,16]{2,1,0:T(8,128)S(1)}, f32[128,16,16]{2,1,0:T(8,128)}, u32[]{:S(2)}) copy-start(f32[128,16,16]{2,1,0:T(8,128)} %copy.51) | copy-start | bytes 393220
  124.6 4.0 copy-start.2
  128.7 4.0 copy-start.3
  132.7 6.5 %copy-start.5 = (f32[128,16,16]{2,1,0:T(8,128)S(1)}, f32[128,16,16]{2,1,0:T(8,128)}, u32[]{:S(2)}) copy-start(f32[128,16,16]{2,1,0:T(8,128)} %copy.48) | copy-start | bytes 393220
  147.3 5.1 %copy-start.12 = (u32[128]{0:T(128)S(1)}, u32[128]{0:T(128)}, u32[]{:S(2)}) copy-start(u32[128]{0:T(128)} %constant.74) | copy-start | bytes 1540
  147.4 110.0 %all-to-all-start.1 = ((bf16[128,1,16,560]{3,2,1,0:T(8,128)(2,1)}), bf16[128,1,16,560]{3,2,1,0:T(8,128)(2,1)}, u32[]{:S(2)}, u32[]{:S(2)}) async-start(bf16[128,1,16,560]{3,2,1,0:T(8,128)(2,1)} %fusion.7), calls=%async_computation.1 | async-start | bytes 5242880 | tf_op jit(solution)/shard_map/all_to_all | solution.py:133
  152.3 252.7 %reduce-scatter.2.cloned.1.call-start = ((), (), s32[]{:S(2)}) async-start(), calls=%async_computation.3 | async-start | bytes 11468800 | tf_op jit(solution)/shard_map/reduce_scatter | solution.py:138
  251.4 6.0 %copy-start.11 = (s32[4]{0:T(128)S(1)}, s32[4]{0:T(128)}, u32[]{:S(2)}) copy-start(s32[4]{0:T(128)} %param.26) | copy-start | bytes 52
  267.9 3.0 copy-start.1
  274.2 5.2 %slice-start = ((s8[4587520]{0:T(1024)(128)(4,1)}), s8[393216]{0:T(1024)(128)(4,1)S(1)}, s32[]{:S(2)}) async-start(s8[4587520]{0:T(1024)(128)(4,1)} %bitcast.116), calls=%async_computation.5 | async-start | bytes 786432
  277.2 2.2 slice-start.1
  289.5 115.5 %copy-start.8 = (f32[2240]{0:T(1024)S(1)}, f32[2240]{0:T(1024)}, u32[]{:S(2)}) copy-start(f32[2240]{0:T(1024)} %param.19) | copy-start | bytes 26884
Sparse Core Ops, SparseCore 0:
  67.0 62.9 all-gather.3
  289.7 115.2 reduce-scatter.1
where the time goes:
time: 423 us; the launch traced here: 417 us
  waiting for transfers between devices  144 us (34%)
  blocking collectives  87.5 us (21%)
  matrix products  76.2 us (18%)
  local copies, waits for them, and re-layouts  49.4 us (12%)
  other arithmetic  30.8 us (7%)
  between operations  14.9 us (4%)
  starting transfers between devices  13.8 us (3%)
    reduce_scatter x1, waiting for transfers between devices, body(): lax.psum_scatter(round_term(jnp.dot(mixed_heads, w_out, preferred_element...  115 us
    unnamed x1, blocking collectives  87.5 us
    all_to_all x1, waiting for transfers between devices, body(): lax.all_to_all(value_tiles, 'tm', split_axis=1, concat_axis=0, tiled=True)  28.4 us
    dot_general x5, matrix products, mix_tiles(): jnp.einsum('fjpq,fjqc->fjpc', matrices[shift_index], sliced, precision=hi...  27.1 us
    dot_general x1, matrix products, body(): jnp.dot(normed, w_value, preferred_element_type=jnp.float32)  10.3 us
    convert_element_type x2, local copies, waits for them, and re-layouts, body(): window.reshape(tok_rows, head_cols).astype(jnp.float32)  10.3 us
    dot_general x1, matrix products, body(): jnp.dot(mixed_heads, w_out, preferred_element_type=jnp.float32)  10.1 us
    dot_general x1, matrix products, body(): jnp.dot(normed, w_key, preferred_element_type=jnp.float32)  9.89 us
  transfers between devices with their start and end apart: 4, of which 2 were waited for; matrix products, arithmetic and copies ran while one was open for 17% of the time, Pallas kernels for 0%

commit v1 on v0

v1 whole, which is shorter than its diff:
```python
import jax
import jax.numpy as jnp
from jax import lax
from jax.experimental import pallas as pl
from jax.experimental.pallas import tpu as pltpu
from jax.sharding import PartitionSpec as P

HD = 112
HP = 128
NH = 5
GW = NH * HP
D = 2240
DP = 2304
HALF = DP // 2
FR = 4
ROWS = 512
TILES = 32
TT = 16
NBR = 8
WIN = 2
EPS = 1e-06
RELS = (0, 2, 3, 1)
MESH = pl.DeviceIdType.MESH
BF = jnp.bfloat16
F32 = jnp.float32

X_GATHER = 0
RING = 3
TWIN = 15
HALO = 18
SCAN = 20
SWAP = 27
MESSAGES = 30


def kernel(
    tok_hbm, scale_ref, shift_ref, gate_ref, wq_hbm, wk_hbm, wv_hbm, wo_hbm, mix_ref,
    decay_ref, last_ref, list_ref, out_hbm,
    tok, resid, raw, wo_raw, wvk, wq, wo, vbuf, kbuf, qbuf, win, mixb, acc,
    sloc, scur, pack_out, pack_in, mixrep, local_sem, send_sem, recv_sem,
):
    tm = lax.axis_index("tm")
    sp = lax.axis_index("space")
    z, y, core = tm // 8, (tm // 2) % 4, tm % 2

    def at(zz, yy, cc):
        return (zz * 8 + yy * 2 + cc, sp)

    def x_peer(step):
        return (tm, (sp + step) % 4)

    def z_peer(step):
        return at((z + step) % 4, y, core)

    def y_peer(step):
        return at(z, (y + step) % 4, core)

    twin = at(z, y, 1 - core)
    right = ((tm + 1) % 32, sp)
    left = ((tm + 31) % 32, sp)
    outer = ((tm + 31 + 2 * core) % 32, sp)

    def remote(number, src, dst, device):
        return pltpu.make_async_remote_copy(
            src_ref=src,
            dst_ref=dst,
            send_sem=send_sem.at[number],
            recv_sem=recv_sem.at[number],
            device_id=device,
            device_id_type=MESH,
        )

    def load(number, src, dst):
        return pltpu.make_async_copy(src, dst, local_sem.at[number])

    load_wo = load(0, wo_hbm, wo_raw)
    load_wv = load(1, wv_hbm, raw.at[0])
    load_wk = load(2, wk_hbm, raw.at[1])
    load_wq = load(3, wq_hbm, raw.at[0])
    load_resid = load(4, tok_hbm.at[pl.ds(pl.multiple_of(sp * ROWS, ROWS), ROWS)], resid)

    def load_tok(f):
        return load(5 + f, tok_hbm.at[pl.ds(f * ROWS, ROWS)], tok.at[f])

    load_wo.start()
    load_wv.start()
    load_tok(0).start()
    load_wk.start()
    for f in range(1, FR):
        load_tok(f).start()
    load_resid.start()

    barrier = pltpu.get_barrier_semaphore()
    partners = [x_peer(i) for i in (1, 2, 3)] + [y_peer(i) for i in (1, 2, 3)]
    partners += [z_peer(i) for i in (1, 2, 3)] + [twin, outer]
    for device in partners:
        pl.semaphore_signal(barrier, inc=1, device_id=device, device_id_type=MESH)
    pl.semaphore_wait(barrier, len(partners))

    load_wo.wait()
    for h in range(NH):
        wo[0, h, 0:HD, 0:D] = wo_raw[h * HD : (h + 1) * HD, :]
        wo[0, h, HD:HP, 0:D] = jnp.zeros((HP - HD, D), BF)
        wo[0, h, :, D:DP] = jnp.zeros((HP, DP - D), BF)

    def columns(c):
        return pl.ds(pl.multiple_of(c * HALF, HALF), HALF)

    def chunk(p, i, first=0, count=32):
        return wo.at[p, :, pl.ds(pl.multiple_of(i * 32 + first, 16), count), columns(core)]

    def place(p):
        return (y, y_peer) if RELS[p] == 2 else (z, z_peer)

    def x_gather(p):
        i, _ = place(p)
        return remote(X_GATHER + p - 1, chunk(0, i), chunk(p, i), x_peer(4 - RELS[p]))

    def ring(p, k):
        i, peer = place(p)
        below, above = (i + 3) % 4, (i + 1) % 4
        if k == 0:
            ref, device = chunk(p, i), peer(1)
        elif k == 1:
            ref, device = chunk(p, i), peer(3)
        elif k == 2:
            ref, device = chunk(p, below, 0, 16), peer(1)
        else:
            ref, device = chunk(p, above, 16, 16), peer(3)
        return remote(RING + (p - 1) * 4 + k, ref, ref, device)

    def to_twin(p):
        ref = wo.at[p, :, :, columns(core)]
        return remote(TWIN + p - 1, ref, ref, twin)

    def ring_first(p):
        x_gather(p).wait_recv()
        ring(p, 0).start()
        ring(p, 1).start()

    def ring_second(p):
        ring(p, 0).wait_recv()
        ring(p, 1).wait_recv()
        ring(p, 2).start()
        ring(p, 3).start()

    def ring_last(p):
        ring(p, 2).wait_recv()
        ring(p, 3).wait_recv()
        to_twin(p).start()

    for p in (2, 3, 1):
        x_gather(p).start()

    def pad_heads(slot, dst, base):
        rows = 160

        def one(i, _):
            r = pl.ds(pl.multiple_of(i * rows, rows), rows)
            part = raw[slot, r, :]
            for h in range(NH):
                dst[r, base + h * HP : base + (h + 1) * HP] = jnp.concatenate(
                    [part[:, h * HD : (h + 1) * HD], jnp.zeros((rows, HP - HD), BF)], axis=1
                )
            return 0

        lax.fori_loop(0, D // rows, one, 0)

    load_wv.wait()
    pad_heads(0, wvk, 0)
    load_wq.start()
    load_wk.wait()
    pad_heads(1, wvk, GW)
    scur[...] = jnp.zeros_like(scur)

    def norm(f):
        rows = 32

        def one(i, _):
            r = pl.ds(pl.multiple_of(i * rows, rows), rows)
            x = tok[f, r, :].astype(F32)
            inverse = lax.rsqrt(jnp.sum(x * x, axis=-1, keepdims=True) * (1.0 / D) + EPS)
            tok[f, r, :] = (x * inverse * (1.0 + scale_ref[...]) + shift_ref[...]).astype(BF)
            return 0

        lax.fori_loop(0, ROWS // rows, one, 0)

    def halo_left():
        return remote(HALO, vbuf.at[pl.ds(2, 2)], vbuf.at[pl.ds(6, 2)], left)

    def halo_right():
        return remote(HALO + 1, vbuf.at[pl.ds(4, 2)], vbuf.at[pl.ds(0, 2)], right)

    def decay(f, h):
        return jnp.exp(jnp.full((1, HP), decay_ref[f, h], F32))

    def frame(f, _):
        load_tok(f).wait()
        norm(f)
        for n in range(2 * GW // 256):
            part = jnp.dot(
                tok[f], wvk[:, n * 256 : (n + 1) * 256], preferred_element_type=F32
            ).astype(BF)
            for half in range(2):
                piece = part[:, half * HP : (half + 1) * HP]
                at_col = n * 256 + half * HP
                if at_col < GW:
                    vbuf[2 + f, :, at_col : at_col + HP] = piece
                else:
                    kbuf[:, at_col - GW : at_col - GW + HP] = piece
        for h in range(NH):
            cols = slice(h * HP, (h + 1) * HP)
            fresh = lax.dot_general(
                kbuf[:, cols], vbuf[2 + f, :, cols], (((0,), (0,)), ((), ())),
                preferred_element_type=F32,
            )
            state = decay(f, h) * scur[h] + fresh
            scur[h] = state
            sloc[f, h] = state

        @pl.when(f == 1)
        def _():
            halo_left().start()
            ring_first(2)
            ring_first(3)

        @pl.when(f == 2)
        def _():
            ring_first(1)

        @pl.when(f == 3)
        def _():
            halo_right().start()

        return 0

    lax.fori_loop(0, FR, frame, 0)

    row_id = lax.broadcasted_iota(jnp.int32, (HP, HP), 0)

    def pack(slot, h, log, state):
        high = log.astype(BF).astype(F32)
        low = log - high
        body = jnp.where(row_id < HD, state, 0.0)
        body = jnp.where(row_id == HD, high, jnp.where(row_id == HD + 1, low, body))
        pack_out[slot, h] = body.astype(BF)

    def unpack(slot, h):
        body = pack_in[slot, h].astype(F32)
        log = body[HD : HD + 1, :] + body[HD + 1 : HD + 2, :]
        return log, jnp.where(row_id < HD, body, 0.0)

    def flag(condition):
        return jnp.where(condition, 1.0, 0.0).astype(F32)

    def join(early, late):
        return early[0] + late[0], jnp.exp(late[0]) * early[1] + late[1]

    def choose(on, pair, other):
        return tuple(on * a + (1.0 - on) * b for a, b in zip(pair, other))

    def masked(on, pair):
        return tuple(on * a for a in pair)

    def own_pair(h):
        log = jnp.full((1, HP), decay_ref[0, h], F32)
        for f in range(1, FR):
            log = log + jnp.full((1, HP), decay_ref[f, h], F32)
        return log, scur[h]

    first_core = flag(core == 0)

    def chip_pair(h):
        own, other = own_pair(h), unpack(0, h)
        return join(choose(first_core, own, other), choose(first_core, other, own))

    def scan_core():
        return remote(SCAN, pack_out.at[0], pack_in.at[0], twin)

    def scan_y(step):
        return remote(SCAN + step, pack_out.at[1], pack_in.at[step], y_peer(step))

    def scan_z(step):
        return remote(SCAN + 3 + step, pack_out.at[2], pack_in.at[3 + step], z_peer(step))

    def row_prefix(h):
        total = None
        for step in (3, 2, 1):
            pair = masked(flag(y >= step), unpack(step, h))
            total = pair if total is None else join(total, pair)
        return total

    def column_prefix(h):
        total = None
        for step in (3, 2, 1):
            pair = masked(flag(z >= step), unpack(3 + step, h))
            total = pair if total is None else join(total, pair)
        return total

    for h in range(NH):
        pack(0, h, *own_pair(h))
    scan_core().start()

    load_wq.wait()
    pad_heads(0, wq, 0)

    def query(f, _):
        for n in range(3):
            width = 256 if n < 2 else 128
            cols = slice(n * 256, n * 256 + width)
            qbuf[f, :, cols] = jnp.dot(
                tok[f], wq[:, cols], preferred_element_type=F32
            ).astype(BF)
        return 0

    scan_core().wait_recv()
    for h in range(NH):
        pack(1, h, *chip_pair(h))
    for step in (1, 2, 3):
        scan_y(step).start()

    lax.fori_loop(0, 2, query, 0)
    ring_second(2)
    ring_second(3)

    for step in (1, 2, 3):
        scan_y(step).wait_recv()
    for h in range(NH):
        total = join(row_prefix(h), chip_pair(h))
        for step in (3, 2, 1):
            total = join(total, masked(flag(y < step), unpack(step, h)))
        pack(2, h, *total)
    for step in (1, 2, 3):
        scan_z(step).start()

    lax.fori_loop(2, FR, query, 0)
    ring_second(1)

    lane = lax.broadcasted_iota(jnp.int32, (TT, HP), 1)
    spread = jnp.where(lane % TT == lax.broadcasted_iota(jnp.int32, (TT, HP), 0), 1.0, 0.0)
    mixrep[...] = jnp.dot(mix_ref[...], spread.astype(BF), preferred_element_type=F32)
    group = lane // TT + (FR * tm - WIN)
    halo_left().wait_recv()
    halo_right().wait_recv()

    def tile(j, _):
        r = pl.ds(pl.multiple_of(j * TT, TT), TT)
        blocks = []
        for f in range(FR):
            block = jnp.zeros((TT, HP), F32)
            for n in range(NBR):
                hit = group == list_ref[(f * TILES + j) * NBR + n]
                block = block + jnp.where(hit, mixrep[n * TT : (n + 1) * TT, :], 0.0)
            blocks.append(block)
        matrix = jnp.concatenate(blocks, axis=0).astype(BF)
        source = vbuf[:, r, :].reshape(2 * FR * TT, GW)
        mixed = jnp.dot(matrix, source, preferred_element_type=F32).astype(BF)
        win[:, r, :] = mixed.reshape(FR, TT, GW)
        return 0

    lax.fori_loop(0, TILES, tile, 0)

    for step in (1, 2, 3):
        scan_z(step).wait_recv()
    for h in range(NH):
        chip = masked(1.0 - first_core, unpack(0, h))
        entering = join(join(column_prefix(h), row_prefix(h)), chip)[1]
        for f in range(FR):
            entering = decay(f, h) * entering
            sloc[f, h] = sloc[f, h] + entering

    def swap(p):
        f = (sp + 4 - RELS[p]) % 4
        return remote(
            SWAP + p - 1, qbuf.at[f], mixb.at[:, pl.ds(p * GW, GW)], x_peer(4 - RELS[p])
        )

    for p in (1, 2, 3, 0):
        f = (sp + 4 - RELS[p]) % 4
        for h in range(NH):
            cols = slice(h * HP, (h + 1) * HP)
            state = jnp.zeros((HP, HP), F32)
            for g in range(FR):
                state = state + flag(last_ref[f] == FR * tm + g) * sloc[g, h]
            state = state.astype(BF)
            for half in range(2):
                r = slice(half * 256, (half + 1) * 256)
                linear = jnp.dot(qbuf[f, r, cols], state, preferred_element_type=F32)
                inverse = lax.rsqrt(
                    jnp.sum(linear * linear, axis=-1, keepdims=True) * (1.0 / HD) + EPS
                )
                both = (linear * inverse + win[f, r, cols].astype(F32)).astype(BF)
                if p == 0:
                    mixb[r, cols] = both
                else:
                    qbuf[f, r, cols] = both
        if p > 0:
            swap(p).start()
        if p == 1:
            ring_last(2)
        if p == 2:
            ring_last(3)
        if p == 3:
            ring_last(1)

    load_resid.wait()
    to_twin(1).wait_recv()
    swap(1).wait_recv()

    def weights(p, cols, width):
        return wo[p : p + 2, :, :, cols].reshape(2 * GW, width)

    def first_part(n, _):
        cols = pl.ds(pl.multiple_of(n * 256, 256), 256)
        acc[:, cols] = jnp.dot(
            mixb[:, 0 : 2 * GW], weights(0, cols, 256), preferred_element_type=F32
        )
        return 0

    lax.fori_loop(0, DP // 256, first_part, 0)

    for p in (2, 3):
        to_twin(p).wait_recv()
        swap(p).wait_recv()

    def finish(cols, width):
        total = acc[:, cols] + jnp.dot(
            mixb[:, 2 * GW : 4 * GW], weights(2, cols, width), preferred_element_type=F32
        )
        resid[:, cols] = (resid[:, cols].astype(F32) + gate_ref[:, cols] * total).astype(BF)

    def second_part(n, _):
        finish(pl.ds(pl.multiple_of(n * 256, 256), 256), 256)
        return 0

    lax.fori_loop(0, D // 256, second_part, 0)
    finish(slice(D // 256 * 256, D), D % 256)
    store = load(9, resid, out_hbm)
    store.start()

    for p in (1, 2, 3):
        x_gather(p).wait_send()
        for k in range(4):
            ring(p, k).wait_send()
        to_twin(p).wait_send()
        swap(p).wait_send()
        scan_y(p).wait_send()
        scan_z(p).wait_send()
    scan_core().wait_send()
    halo_left().wait_send()
    halo_right().wait_send()
    store.wait()


def body(
    tokens, mod_scale, mod_shift, out_gate, w_query, w_key, w_value, w_out,
    log_decay, mix_weight, block_last, win_list,
):
    lists = lax.dynamic_slice_in_dim(win_list, lax.axis_index("tm") * FR, FR, 0).reshape(-1)
    anywhere = pl.BlockSpec(memory_space=pl.ANY)
    vmem = pl.BlockSpec(memory_space=pltpu.VMEM)
    smem = pl.BlockSpec(memory_space=pltpu.SMEM)
    return pl.pallas_call(
        kernel,
        out_shape=jax.ShapeDtypeStruct((ROWS, D), BF),
        in_specs=[anywhere, vmem, vmem, vmem] + [anywhere] * 4 + [vmem, smem, smem, smem],
        out_specs=anywhere,
        scratch_shapes=[
            pltpu.VMEM((FR, ROWS, D), BF),
            pltpu.VMEM((ROWS, D), BF),
            pltpu.VMEM((2, D, NH * HD), BF),
            pltpu.VMEM((NH * HD, D), BF),
            pltpu.VMEM((D, 2 * GW), BF),
            pltpu.VMEM((D, GW), BF),
            pltpu.VMEM((4, NH, HP, DP), BF),
            pltpu.VMEM((2 * FR, ROWS, GW), BF),
            pltpu.VMEM((ROWS, GW), BF),
            pltpu.VMEM((FR, ROWS, GW), BF),
            pltpu.VMEM((FR, ROWS, GW), BF),
            pltpu.VMEM((ROWS, 4 * GW), BF),
            pltpu.VMEM((ROWS, DP), F32),
            pltpu.VMEM((FR, NH, HP, HP), F32),
            pltpu.VMEM((NH, HP, HP), F32),
            pltpu.VMEM((3, NH, HP, HP), BF),
            pltpu.VMEM((7, NH, HP, HP), BF),
            pltpu.VMEM((NBR * TT, HP), F32),
            pltpu.SemaphoreType.DMA((10,)),
            pltpu.SemaphoreType.DMA((MESSAGES,)),
            pltpu.SemaphoreType.DMA((MESSAGES,)),
        ],
        compiler_params=pltpu.CompilerParams(
            collective_id=0, has_side_effects=True, vmem_limit_bytes=66_000_000
        ),
    )(
        tokens,
        mod_scale.reshape(1, D),
        mod_shift.reshape(1, D),
        out_gate.reshape(1, D),
        w_query,
        w_key,
        w_value,
        w_out,
        mix_weight.reshape(NBR * TT, TT),
        log_decay,
        block_last,
        lists,
    )


def solution(mesh):
    placed = (
        P("tm", None),
        P(),
        P(),
        P(),
        P(None, "space"),
        P(None, "space"),
        P(None, "space"),
        P("space", None),
        P("tm", "space"),
        P(),
        P("tm"),
        P(),
    )
    return jax.shard_map(
        body, mesh=mesh, in_specs=placed, out_specs=P(("tm", "space"), None), check_vma=False
    )
```

time: 423 us -> 147 us (0.35); the launches traced: 417 us -> 145 us
  waiting for transfers between devices: 144 us -> 0 us
  Pallas kernels: 0 us -> 111 us
  blocking collectives: 87.5 us -> 0 us
  matrix products: 76.2 us -> 0 us
  other arithmetic: 30.8 us -> 0 us
  local copies, waits for them, and re-layouts: 49.4 us -> 33.9 us
  between operations: 14.9 us -> 0.03 us
  starting transfers between devices: 13.8 us -> 0 us
    reduce_scatter x1 -> x0, waiting for transfers between devices: 115 us -> none  [body(): lax.psum_scatter(round_term(jnp.dot(mixed_heads, w_out, preferred_element...]
    pallas_call x0 -> x1, Pallas kernels: none -> 111 us  [body(): pl.pallas_call(kernel, out_shape=jax.ShapeDtypeStruct((ROWS, D), BF), in_...]
    unnamed x1 -> x0, blocking collectives: 87.5 us -> none
    dot_general x13 -> x0, matrix products: 76.2 us -> none  [the longest x5 27.1 us: mix_tiles(): jnp.einsum('fjpq,fjqc->fjpc', matrices[shift_index], sliced, precision=hi...]
    all_to_all x2 -> x0, waiting for transfers between devices: 28.4 us -> none  [the longest x1 28.4 us: body(): lax.all_to_all(value_tiles, 'tm', split_axis=1, concat_axis=0, tiled=True)]
    unnamed x34 -> x8, local copies, waits for them, and re-layouts: 3.11 us -> 24.6 us
    reshape x4, local copies, waits for them, and re-layouts: 21.6 us -> 4.65 us  [the longest x1 1.35 us: body(): mod_scale.reshape(1, D)]
    convert_element_type x3 -> x0, other arithmetic: 15 us -> none  [the longest x1 9.87 us: body(): (unit_rms(tokens.astype(jnp.float32)) * (1.0 + mod_scale) + mod_shift).as...]
  transfers between devices with their start and end apart: 4 -> 0, of which waited for: 2 -> 0; matrix products, arithmetic and copies ran while one was open for 17% -> 0% of each run, Pallas kernels for 0% -> 0%
where the time goes in v1:
time: 147 us; the launch traced here: 145 us
  Pallas kernels  111 us (76%)
  local copies, waits for them, and re-layouts  33.9 us (23%)
    pallas_call x1, Pallas kernels, body(): pl.pallas_call(kernel, out_shape=jax.ShapeDtypeStruct((ROWS, D), BF), in_...  111 us
    unnamed x8, local copies, waits for them, and re-layouts  24.6 us
    pallas_call x1, local copies, waits for them, and re-layouts, body(): pl.pallas_call(kernel, out_shape=jax.ShapeDtypeStruct((ROWS, D), BF), in_...  4.26 us

profile of v1, /device:TPU:0, one launch (start us, length us, event | category | flops | bytes accessed | tf_op | source)
XLA Modules:
  0.0 145.1 jit_solution(8205729838675692738)
XLA Ops:
  0.0 0.0 copy-start
  0.0 1.3 reshape.15.scale_ref
  1.4 1.3 reshape.16.shift_ref
  2.7 1.3 reshape.17.gate_ref
  4.0 0.0 copy-done
  4.0 0.1 constant_dynamic-slice_fusion
  4.1 0.3 copy.18
  4.4 0.7 reshape.19.list_ref
  5.1 0.0 copy-start.1
  5.1 4.6 %copy.20.wq_hbm = bf16[2240,560]{1,0:T(8,128)(2,1)} copy(bf16[2240,560]{0,1:T(8,128)(2,1)} %param.16) | data formatting | bytes 5017600 | tf_op args[4]
  9.7 0.0 copy-done.1
  9.7 2.9 %copy.21.wk_hbm = bf16[2240,560]{1,0:T(8,128)(2,1)} copy(bf16[2240,560]{0,1:T(8,128)(2,1)S(1)} %copy-done.1) | data formatting | bytes 5017600 | tf_op args[5]
  12.6 4.5 %copy.22.wv_hbm = bf16[2240,560]{1,0:T(8,128)(2,1)} copy(bf16[2240,560]{0,1:T(8,128)(2,1)} %param.18) | data formatting | bytes 5017600 | tf_op args[6]
  17.1 12.5 %copy.19.tok_hbm = bf16[2048,2240]{1,0:T(8,128)(2,1)} copy(bf16[2048,2240]{0,1:T(8,128)(2,1)} %param.12) | data formatting | bytes 18350080 | tf_op args[0]
  29.6 111.2 %shard_map.118 = bf16[512,2240]{1,0:T(8,128)(2,1)} custom-call(bf16[2048,2240]{1,0:T(8,128)(2,1)} %copy.19.tok_hbm, f32[1,2240]{1,0:T(1,128)} %reshape.15.scale_ref, f32[1,2240]{1,0:T(1,128)} %reshape.16.shift_ref, f32[1,2240]{1,0:T(1,128)} %reshape.17.gate_ref, bf16[2240,560]{1,0:T(8,128)(2,1)} %copy.20.wq_hbm, bf16[2240,560]{1,0:T(8,128)(2,1)} %copy.21.wk_hbm, ...), custom_call_target="tpu_custom_call" | custom-call | tf_op jit(solution)/shard_map/pallas_call | solution.py:463
  140.8 4.3 %copy.23 = bf16[512,2240]{0,1:T(8,128)(2,1)} copy(bf16[512,2240]{1,0:T(8,128)(2,1)} %shard_map.118) | data formatting | bytes 4587520 | tf_op jit(solution)/shard_map/pallas_call | solution.py:463
Async XLA Ops:
  0.0 4.0 %copy-start = (s32[128,32,8]{0,2,1:T(8,128)S(1)}, s32[128,32,8]{0,2,1:T(8,128)}, u32[]{:S(2)}) copy-start(s32[128,32,8]{0,2,1:T(8,128)} %param.23) | copy-start | bytes 393220
  5.1 4.6 %copy-start.1 = (bf16[2240,560]{0,1:T(8,128)(2,1)S(1)}, bf16[2240,560]{0,1:T(8,128)(2,1)}, u32[]{:S(2)}) copy-start(bf16[2240,560]{0,1:T(8,128)(2,1)} %param.17) | copy-start | bytes 7526404

commit v2 on v1

v2 whole, which is shorter than its diff:
```python
import jax
import jax.numpy as jnp
from jax import lax
from jax.experimental import pallas as pl
from jax.experimental.pallas import tpu as pltpu
from jax.sharding import PartitionSpec as P

HD = 112
NH = 5
GW = NH * HD
GP = 640
D = 2240
FR = 4
ROWS = 512
TILES = 32
TT = 16
NBR = 8
WIN = 2
PART = 288
EPS = 1e-06
RELS = (0, 2, 3, 1)
MESH = pl.DeviceIdType.MESH
BF = jnp.bfloat16
F32 = jnp.float32
NT = (((1,), (1,)), ((), ()))

X_GATHER = 0
RING = 3
TWIN = 15
HALO = 18
SCAN = 20
SWAP = 27
MESSAGES = 30


def kernel(
    tok_hbm, scale_ref, shift_ref, gate_ref, wq_hbm, wk_hbm, wv_hbm, wo_hbm, mix_ref,
    decay_ref, last_ref, list_ref, out_hbm,
    tok, resid, wqkv, wo_raw, wo, vbuf, kbuf, qbuf, win, mixb, acc, gains,
    sloc, scur, pack_out, pack_in, mixrep, rel, band, local_sem, send_sem, recv_sem,
):
    tm = lax.axis_index("tm")
    sp = lax.axis_index("space")
    z, y, core = tm // 8, (tm // 2) % 4, tm % 2

    def at(zz, yy, cc):
        return (zz * 8 + yy * 2 + cc, sp)

    def x_peer(step):
        return (tm, (sp + step) % 4)

    def z_peer(step):
        return at((z + step) % 4, y, core)

    def y_peer(step):
        return at(z, (y + step) % 4, core)

    twin = at(z, y, 1 - core)
    right = ((tm + 1) % 32, sp)
    left = ((tm + 31) % 32, sp)
    outer = ((tm + 31 + 2 * core) % 32, sp)

    def remote(number, src, dst, device):
        return pltpu.make_async_remote_copy(
            src_ref=src,
            dst_ref=dst,
            send_sem=send_sem.at[number],
            recv_sem=recv_sem.at[number],
            device_id=device,
            device_id_type=MESH,
        )

    def load(number, src, dst):
        return pltpu.make_async_copy(src, dst, local_sem.at[number])

    load_wo = load(0, wo_hbm, wo_raw.at[pl.ds(0, GW)])
    load_wv = load(1, wv_hbm, wqkv.at[0])
    load_wk = load(2, wk_hbm, wqkv.at[1])
    load_wq = load(3, wq_hbm, wqkv.at[2])
    own_rows = pl.ds(pl.multiple_of(sp * ROWS, ROWS), ROWS)
    load_resid = load(4, tok_hbm.at[:, own_rows], resid)

    def load_tok(f):
        rows = pl.ds(pl.multiple_of(f * ROWS, ROWS), ROWS)
        return load(5 + f, tok_hbm.at[:, rows], tok.at[f])

    load_wo.start()
    load_tok(0).start()
    load_wv.start()
    for f in range(1, FR):
        load_tok(f).start()
    load_wk.start()
    load_wq.start()
    load_resid.start()

    barrier = pltpu.get_barrier_semaphore()
    partners = [x_peer(i) for i in (1, 2, 3)] + [y_peer(i) for i in (1, 2, 3)]
    partners += [z_peer(i) for i in (1, 2, 3)] + [twin, outer]
    for device in partners:
        pl.semaphore_signal(barrier, inc=1, device_id=device, device_id_type=MESH)

    for k, vector in enumerate((scale_ref, shift_ref, gate_ref)):
        for low in range(0, D, 128):
            high = min(low + 128, D)
            row = vector[pl.ds(low, high - low)].reshape(1, high - low)
            column = jnp.broadcast_to(row, (128, high - low)).T
            gains[k, low:high, :] = 1.0 + column if k == 0 else column

    def spots(rows, lanes, of_row, of_lane):
        r = lax.broadcasted_iota(jnp.int32, (rows, lanes), 0)
        l = lax.broadcasted_iota(jnp.int32, (rows, lanes), 1)
        return jnp.where(of_row(r) == of_lane(l), 1.0, 0.0).astype(BF)

    def exact(a, b, dims=(((1,), (0,)), ((), ()))):
        return lax.dot_general(a, b, dims, preferred_element_type=F32)

    mixed_t = exact(spots(TT, TT, lambda r: r, lambda l: l), mix_ref[...], NT).astype(BF)
    mine = exact(
        spots(8, 128, lambda r: r + FR * tm, lambda l: l), list_ref[...].astype(BF), NT
    )
    mine = (mine - (FR * tm - WIN).astype(F32)).astype(BF)
    for n in range(NBR):
        mixrep[n] = exact(
            mixed_t, spots(128, 128, lambda r: r, lambda l: l % TT + n * TT)
        )
        rel[n] = exact(
            mine, spots(TILES * NBR, ROWS, lambda r: r, lambda l: l // TT * NBR + n)
        )
    band[...] = jnp.zeros_like(band)
    for p in range(4):
        mixb[p * GP + GW : (p + 1) * GP, :] = jnp.zeros((GP - GW, ROWS), BF)

    wo_raw[GW:GP, :] = jnp.zeros((GP - GW, D), BF)
    wo[3, 1, D - 7 * PART : PART, 0:GP] = jnp.zeros((8 * PART - D, GP), BF)
    load_wo.wait()
    for low in range(0, D, 256):
        high = min(low + 256, D)
        eye = spots(high - low, high - low, lambda r: r, lambda l: l)
        turned = exact(eye, wo_raw[:, low:high], NT).astype(BF)
        for part in range(8):
            first, last = max(low, part * PART), min(high, (part + 1) * PART)
            if first < last:
                wo[part // 2, part % 2, first - part * PART : last - part * PART, 0:GP] = turned[
                    first - low : last - low
                ]

    pl.semaphore_wait(barrier, len(partners))

    def chunk(p, i, first=0, count=PART):
        return wo.at[i, core, pl.ds(first, count), pl.ds(p * GP, GP)]

    def place(p):
        return (y, y_peer) if RELS[p] == 2 else (z, z_peer)

    def x_gather(p):
        i, _ = place(p)
        return remote(X_GATHER + p - 1, chunk(0, i), chunk(p, i), x_peer(4 - RELS[p]))

    def ring(p, k):
        i, peer = place(p)
        below, above = (i + 3) % 4, (i + 1) % 4
        if k == 0:
            ref, device = chunk(p, i), peer(1)
        elif k == 1:
            ref, device = chunk(p, i), peer(3)
        elif k == 2:
            ref, device = chunk(p, below, 0, PART // 2), peer(1)
        else:
            ref, device = chunk(p, above, PART // 2, PART // 2), peer(3)
        return remote(RING + (p - 1) * 4 + k, ref, ref, device)

    def to_twin(p):
        ref = wo.at[:, core, :, pl.ds(p * GP, GP)]
        return remote(TWIN + p - 1, ref, ref, twin)

    def ring_first(p):
        x_gather(p).wait_recv()
        ring(p, 0).start()
        ring(p, 1).start()

    def ring_second(p):
        ring(p, 0).wait_recv()
        ring(p, 1).wait_recv()
        ring(p, 2).start()
        ring(p, 3).start()

    def ring_last(p):
        ring(p, 2).wait_recv()
        ring(p, 3).wait_recv()
        to_twin(p).start()

    for p in (2, 3, 1):
        x_gather(p).start()

    def norm(f):
        rows = 32

        def squares(i, total):
            x = tok[f, pl.ds(pl.multiple_of(i * rows, rows), rows), :].astype(F32)
            return total + jnp.sum((x * x).reshape(rows // 8, 8, ROWS), axis=0)

        total = lax.fori_loop(0, D // rows, squares, jnp.zeros((8, ROWS), F32), unroll=2)
        inverse = lax.rsqrt(jnp.sum(total, axis=0, keepdims=True) * (1.0 / D) + EPS)

        def scale(i, _):
            r = pl.ds(pl.multiple_of(i * rows, rows), rows)
            gain, shift = gains[0, r, :], gains[1, r, :]
            for c in range(ROWS // 128):
                cols = slice(c * 128, (c + 1) * 128)
                x = tok[f, r, cols].astype(F32)
                tok[f, r, cols] = (x * inverse[:, cols] * gain + shift).astype(BF)
            return 0

        lax.fori_loop(0, D // rows, scale, 0, unroll=2)

    def halo_left():
        return remote(HALO, vbuf.at[pl.ds(2, 2)], vbuf.at[pl.ds(6, 2)], left)

    def halo_right():
        return remote(HALO + 1, vbuf.at[pl.ds(4, 2)], vbuf.at[pl.ds(0, 2)], right)

    def decay(f, h):
        return jnp.exp(jnp.full((1, HD), decay_ref[f, h], F32))

    def project(weight, f, dst):
        for half in range(2):
            cols = slice(half * 256, (half + 1) * 256)
            dst[:, cols] = jnp.dot(
                wqkv[weight], tok[f, :, cols], preferred_element_type=F32
            ).astype(BF)

    load_wv.wait()

    def value(f, _):
        load_tok(f).wait()
        norm(f)
        project(0, f, vbuf.at[2 + f])

        @pl.when(f == 1)
        def _():
            halo_left().start()

        @pl.when(f == 3)
        def _():
            halo_right().start()

        return 0

    lax.fori_loop(0, FR, value, 0)
    ring_first(2)
    ring_first(3)

    load_wk.wait()
    scur[...] = jnp.zeros_like(scur)

    def key(f, _):
        project(1, f, kbuf)
        for h in range(NH):
            rows = slice(h * HD, (h + 1) * HD)
            fresh = exact(vbuf[2 + f, rows, :], kbuf[rows, :], NT)
            state = decay(f, h) * scur[h] + fresh
            scur[h] = state
            sloc[f, h] = state
        return 0

    lax.fori_loop(0, FR, key, 0)

    row_id = lax.broadcasted_iota(jnp.int32, (TT, HD), 0)

    def pack(slot, h, log, state):
        high = log.astype(BF).astype(F32)
        low = log - high
        tail = jnp.where(row_id == 0, high, jnp.where(row_id == 1, low, 0.0))
        pack_out[slot, h, 0:HD, :] = state.astype(BF)
        pack_out[slot, h, HD:128, :] = tail.astype(BF)

    def unpack(slot, h):
        tail = pack_in[slot, h, HD:128, :].astype(F32)
        return jnp.sum(tail, axis=0, keepdims=True), pack_in[slot, h, 0:HD, :].astype(F32)

    def flag(condition):
        return jnp.where(condition, 1.0, 0.0).astype(F32)

    def join(early, late):
        return early[0] + late[0], jnp.exp(late[0]) * early[1] + late[1]

    def choose(on, pair, other):
        return tuple(on * a + (1.0 - on) * b for a, b in zip(pair, other))

    def masked(on, pair):
        return tuple(on * a for a in pair)

    def own_pair(h):
        log = jnp.full((1, HD), decay_ref[0, h], F32)
        for f in range(1, FR):
            log = log + jnp.full((1, HD), decay_ref[f, h], F32)
        return log, scur[h]

    first_core = flag(core == 0)

    def chip_pair(h):
        own, other = own_pair(h), unpack(0, h)
        return join(choose(first_core, own, other), choose(first_core, other, own))

    def scan_core():
        return remote(SCAN, pack_out.at[0], pack_in.at[0], twin)

    def scan_y(step):
        return remote(SCAN + step, pack_out.at[1], pack_in.at[step], y_peer(step))

    def scan_z(step):
        return remote(SCAN + 3 + step, pack_out.at[2], pack_in.at[3 + step], z_peer(step))

    def row_prefix(h):
        total = None
        for step in (3, 2, 1):
            pair = masked(flag(y >= step), unpack(step, h))
            total = pair if total is None else join(total, pair)
        return total

    def column_prefix(h):
        total = None
        for step in (3, 2, 1):
            pair = masked(flag(z >= step), unpack(3 + step, h))
            total = pair if total is None else join(total, pair)
        return total

    for h in range(NH):
        pack(0, h, *own_pair(h))
    scan_core().start()

    load_wq.wait()

    def query(f, _):
        project(2, f, qbuf.at[f])
        return 0

    ring_first(1)
    scan_core().wait_recv()
    for h in range(NH):
        pack(1, h, *chip_pair(h))
    for step in (1, 2, 3):
        scan_y(step).start()

    lax.fori_loop(0, 2, query, 0)
    ring_second(2)
    ring_second(3)

    for step in (1, 2, 3):
        scan_y(step).wait_recv()
    for h in range(NH):
        total = join(row_prefix(h), chip_pair(h))
        for step in (3, 2, 1):
            total = join(total, masked(flag(y < step), unpack(step, h)))
        pack(2, h, *total)
    for step in (1, 2, 3):
        scan_z(step).start()

    lax.fori_loop(2, FR, query, 0)
    ring_second(1)

    halo_left().wait_recv()
    halo_right().wait_recv()
    tile_of_lane = lax.broadcasted_iota(jnp.int32, (TT, 128), 1) // TT

    def tiles(j, _):
        cols = pl.ds(pl.multiple_of(j * 128, 128), 128)
        for pair in range(2):
            for f in range(2):
                for g in range(f, f + 2 * WIN + 1):
                    block = jnp.zeros((TT, 128), F32)
                    for n in range(NBR):
                        listed = rel[n, pl.ds(2 * pair + f, 1), cols]
                        block = block + jnp.where(listed == 2 * pair + g, mixrep[n], 0.0)
                    for t in range(8):
                        low = g * 128 + t * TT
                        band[pair, low : low + TT, f * 128 : (f + 1) * 128] = jnp.where(
                            tile_of_lane == t, block, 0.0
                        ).astype(BF)
            source = jnp.concatenate(
                [vbuf[2 * pair + g, :, cols] for g in range(2 * WIN + 2)], axis=1
            )
            mixed = exact(source, band[pair]).astype(BF)
            for f in range(2):
                win[2 * pair + f, :, cols] = mixed[:, f * 128 : (f + 1) * 128]
        return 0

    lax.fori_loop(0, ROWS // 128, tiles, 0)

    for step in (1, 2, 3):
        scan_z(step).wait_recv()
    for h in range(NH):
        chip = masked(1.0 - first_core, unpack(0, h))
        entering = join(join(column_prefix(h), row_prefix(h)), chip)[1]
        for f in range(FR):
            entering = decay(f, h) * entering
            sloc[f, h] = sloc[f, h] + entering

    def swap(p):
        f = (sp + 4 - RELS[p]) % 4
        return remote(
            SWAP + p - 1, qbuf.at[f], mixb.at[pl.ds(p * GP, GW)], x_peer(4 - RELS[p])
        )

    for p in (1, 2, 3, 0):
        f = (sp + 4 - RELS[p]) % 4
        for h in range(NH):
            rows = slice(h * HD, (h + 1) * HD)
            state = jnp.zeros((HD, HD), F32)
            for g in range(FR):
                state = state + flag(last_ref[f] == FR * tm + g) * sloc[g, h]
            linear = exact(state.astype(BF), qbuf[f, rows, :])
            inverse = lax.rsqrt(
                jnp.sum(linear * linear, axis=0, keepdims=True) * (1.0 / HD) + EPS
            )
            both = (linear * inverse + win[f, rows, :].astype(F32)).astype(BF)
            if p == 0:
                mixb[rows, :] = both
            else:
                qbuf[f, rows, :] = both
        if p > 0:
            swap(p).start()
        if p == 1:
            ring_last(2)
        if p == 2:
            ring_last(3)
        if p == 3:
            ring_last(1)

    load_resid.wait()

    def weights(i, p, count):
        return wo[i, :, :, p * GP : (p + count) * GP].reshape(2 * PART, count * GP)

    for i in range(4):
        low, high = i * 2 * PART, min((i + 1) * 2 * PART, D)
        acc[low:high, :] = exact(weights(i, 0, 1)[: high - low], mixb[0:GP, :])

    to_twin(1).wait_recv()
    swap(1).wait_recv()
    for i in range(4):
        low, high = i * 2 * PART, min((i + 1) * 2 * PART, D)
        acc[low:high, :] += exact(weights(i, 1, 1)[: high - low], mixb[GP : 2 * GP, :])

    for p in (2, 3):
        to_twin(p).wait_recv()
        swap(p).wait_recv()
    for i in range(4):
        low, high = i * 2 * PART, min((i + 1) * 2 * PART, D)
        total = acc[low:high, :] + exact(weights(i, 2, 2)[: high - low], mixb[2 * GP : 4 * GP, :])
        for c in range(ROWS // 128):
            cols = slice(c * 128, (c + 1) * 128)
            resid[low:high, cols] = (
                resid[low:high, cols].astype(F32) + gains[2, low:high, :] * total[:, cols]
            ).astype(BF)
    store = load(9, resid, out_hbm)
    store.start()

    for p in (1, 2, 3):
        x_gather(p).wait_send()
        for k in range(4):
            ring(p, k).wait_send()
        to_twin(p).wait_send()
        swap(p).wait_send()
        scan_y(p).wait_send()
        scan_z(p).wait_send()
    scan_core().wait_send()
    halo_left().wait_send()
    halo_right().wait_send()
    store.wait()


def body(
    tokens, mod_scale, mod_shift, out_gate, w_query, w_key, w_value, w_out,
    log_decay, mix_weight, block_last, win_list,
):
    anywhere = pl.BlockSpec(memory_space=pl.ANY)
    vmem = pl.BlockSpec(memory_space=pltpu.VMEM)
    smem = pl.BlockSpec(memory_space=pltpu.SMEM)
    out = pl.pallas_call(
        kernel,
        out_shape=jax.ShapeDtypeStruct((D, ROWS), BF),
        in_specs=[anywhere, vmem, vmem, vmem] + [anywhere] * 4 + [vmem, smem, smem, vmem],
        out_specs=anywhere,
        scratch_shapes=[
            pltpu.VMEM((FR, D, ROWS), BF),
            pltpu.VMEM((D, ROWS), BF),
            pltpu.VMEM((3, GW, D), BF),
            pltpu.VMEM((GP, D), BF),
            pltpu.VMEM((4, 2, PART, 4 * GP), BF),
            pltpu.VMEM((2 * FR, GW, ROWS), BF),
            pltpu.VMEM((GW, ROWS), BF),
            pltpu.VMEM((FR, GW, ROWS), BF),
            pltpu.VMEM((FR, GW, ROWS), BF),
            pltpu.VMEM((4 * GP, ROWS), BF),
            pltpu.VMEM((D, ROWS), F32),
            pltpu.VMEM((3, D, 128), F32),
            pltpu.VMEM((FR, NH, HD, HD), F32),
            pltpu.VMEM((NH, HD, HD), F32),
            pltpu.VMEM((3, NH, 128, HD), BF),
            pltpu.VMEM((7, NH, 128, HD), BF),
            pltpu.VMEM((NBR, TT, 128), F32),
            pltpu.VMEM((NBR, 8, ROWS), F32),
            pltpu.VMEM((2, (2 * WIN + 2) * 128, 256), BF),
            pltpu.SemaphoreType.DMA((10,)),
            pltpu.SemaphoreType.DMA((MESSAGES,)),
            pltpu.SemaphoreType.DMA((MESSAGES,)),
        ],
        compiler_params=pltpu.CompilerParams(
            collective_id=0, has_side_effects=True, vmem_limit_bytes=66_000_000
        ),
    )(
        tokens.T,
        mod_scale,
        mod_shift,
        out_gate,
        w_query.T,
        w_key.T,
        w_value.T,
        w_out,
        mix_weight.reshape(NBR * TT, TT),
        log_decay,
        block_last,
        win_list.transpose(1, 2, 0).reshape(TILES * NBR, -1),
    )
    return out.T


def solution(mesh):
    placed = (
        P("tm", None),
        P(),
        P(),
        P(),
        P(None, "space"),
        P(None, "space"),
        P(None, "space"),
        P("space", None),
        P("tm", "space"),
        P(),
        P("tm"),
        P(),
    )
    return jax.shard_map(
        body, mesh=mesh, in_specs=placed, out_specs=P(("tm", "space"), None), check_vma=False
    )
```

time: 147 us -> 102 us (0.69)
  local copies, waits for them, and re-layouts: 33.9 us -> 3.18 us
  Pallas kernels: 111 us -> 98 us
    unnamed x8 -> x1, local copies, waits for them, and re-layouts: 24.6 us -> 3.18 us
    pallas_call x1, Pallas kernels: 111 us -> 98 us  [body(): pl.pallas_call(kernel, out_shape=jax.ShapeDtypeStruct((D, ROWS), BF), in_...]
    reshape x4 -> x0, local copies, waits for them, and re-layouts: 4.65 us -> none  [the longest x1 1.35 us: body(): mod_scale.reshape(1, D)]
    pallas_call x1 -> x0, local copies, waits for them, and re-layouts: 4.26 us -> none  [body(): pl.pallas_call(kernel, out_shape=jax.ShapeDtypeStruct((ROWS, D), BF), in_...]
where the time goes in v2:
time: 102 us; the launch traced here: 101 us
  Pallas kernels  98 us (96%)
  local copies, waits for them, and re-layouts  3.18 us (3%)
    pallas_call x1, Pallas kernels, body(): pl.pallas_call(kernel, out_shape=jax.ShapeDtypeStruct((D, ROWS), BF), in_...  98 us
    unnamed x1, local copies, waits for them, and re-layouts  3.18 us

profile of v2, /device:TPU:0, one launch (start us, length us, event | category | flops | bytes accessed | tf_op | source)
XLA Modules:
  0.0 101.2 jit_solution(2407616359847006602)
XLA Ops:
  0.0 98.0 %shard_map.118 = bf16[2240,512]{1,0:T(8,128)(2,1)} custom-call(bf16[2240,2048]{1,0:T(8,128)(2,1)} %bitcast.9, f32[2240]{0:T(1024)} %scale_ref.1, f32[2240]{0:T(1024)} %shift_ref.1, f32[2240]{0:T(1024)} %gate_ref.1, bf16[560,2240]{1,0:T(8,128)(2,1)} %bitcast.11, bf16[560,2240]{1,0:T(8,128)(2,1)} %bitcast.12, bf16[560,2240]{1,0:T(8,128)(2,1)} %bitcast.13, ...), custom_call_target="tpu_custom_call" | custom-call | tf_op jit(solution)/shard_map/pallas_call | solution.py:480
  98.0 3.2 %copy.14 = bf16[512,2240]{0,1:T(8,128)(2,1)} copy(bf16[512,2240]{0,1:T(8,128)(2,1)} %bitcast.10) | data formatting | bytes 4587520

commit v3 on v2

--- a/solution.py
+++ b/solution.py
@@ -25,19 +25,21 @@
 NT = (((1,), (1,)), ((), ()))
 
 X_GATHER = 0
-RING = 3
-TWIN = 15
-HALO = 18
-SCAN = 20
-SWAP = 27
-MESSAGES = 30
+RING = 5
+TWIN = 13
+HALO = 16
+SCAN = 18
+SWAP = 26
+MESSAGES = 29
+HALF = 64
 
 
 def kernel(
     tok_hbm, scale_ref, shift_ref, gate_ref, wq_hbm, wk_hbm, wv_hbm, wo_hbm, mix_ref,
     decay_ref, last_ref, list_ref, out_hbm,
     tok, resid, wqkv, wo_raw, wo, vbuf, kbuf, qbuf, win, mixb, acc, gains,
-    sloc, scur, pack_out, pack_in, mixrep, rel, band, local_sem, send_sem, recv_sem,
+    sloc, scur, entry, full_out, full_in, half_out, half_in, end_out, end_in,
+    mixrep, rel, band, local_sem, send_sem, recv_sem,
 ):
     tm = lax.axis_index("tm")
     sp = lax.axis_index("space")
@@ -99,13 +101,6 @@
     for device in partners:
         pl.semaphore_signal(barrier, inc=1, device_id=device, device_id_type=MESH)
 
-    for k, vector in enumerate((scale_ref, shift_ref, gate_ref)):
-        for low in range(0, D, 128):
-            high = min(low + 128, D)
-            row = vector[pl.ds(low, high - low)].reshape(1, high - low)
-            column = jnp.broadcast_to(row, (128, high - low)).T
-            gains[k, low:high, :] = 1.0 + column if k == 0 else column
-
     def spots(rows, lanes, of_row, of_lane):
         r = lax.broadcasted_iota(jnp.int32, (rows, lanes), 0)
         l = lax.broadcasted_iota(jnp.int32, (rows, lanes), 1)
@@ -114,19 +109,6 @@
     def exact(a, b, dims=(((1,), (0,)), ((), ()))):
         return lax.dot_general(a, b, dims, preferred_element_type=F32)
 
-    mixed_t = exact(spots(TT, TT, lambda r: r, lambda l: l), mix_ref[...], NT).astype(BF)
-    mine = exact(
-        spots(8, 128, lambda r: r + FR * tm, lambda l: l), list_ref[...].astype(BF), NT
-    )
-    mine = (mine - (FR * tm - WIN).astype(F32)).astype(BF)
-    for n in range(NBR):
-        mixrep[n] = exact(
-            mixed_t, spots(128, 128, lambda r: r, lambda l: l % TT + n * TT)
-        )
-        rel[n] = exact(
-            mine, spots(TILES * NBR, ROWS, lambda r: r, lambda l: l // TT * NBR + n)
-        )
-    band[...] = jnp.zeros_like(band)
     for p in range(4):
         mixb[p * GP + GW : (p + 1) * GP, :] = jnp.zeros((GP - GW, ROWS), BF)
 
@@ -149,48 +131,47 @@
     def chunk(p, i, first=0, count=PART):
         return wo.at[i, core, pl.ds(first, count), pl.ds(p * GP, GP)]
 
-    def place(p):
-        return (y, y_peer) if RELS[p] == 2 else (z, z_peer)
-
-    def x_gather(p):
-        i, _ = place(p)
-        return remote(X_GATHER + p - 1, chunk(0, i), chunk(p, i), x_peer(4 - RELS[p]))
-
-    def ring(p, k):
-        i, peer = place(p)
-        below, above = (i + 3) % 4, (i + 1) % 4
+    def x_gather(p, second=0):
+        i = y if p == 1 else (z + second) % 4
+        number = X_GATHER + p - 1 + 2 * second
+        return remote(number, chunk(0, i), chunk(p, i), x_peer(4 - RELS[p]))
+
+    def y_ring(k):
+        below, above = (y + 3) % 4, (y + 1) % 4
         if k == 0:
-            ref, device = chunk(p, i), peer(1)
+            ref, device = chunk(1, y), y_peer(1)
         elif k == 1:
-            ref, device = chunk(p, i), peer(3)
+            ref, device = chunk(1, y), y_peer(3)
         elif k == 2:
-            ref, device = chunk(p, below, 0, PART // 2), peer(1)
+            ref, device = chunk(1, below, 0, PART // 2), y_peer(1)
         else:
-            ref, device = chunk(p, above, PART // 2, PART // 2), peer(3)
-        return remote(RING + (p - 1) * 4 + k, ref, ref, device)
+            ref, device = chunk(1, above, PART // 2, PART // 2), y_peer(3)
+        return remote(RING + k, ref, ref, device)
+
+    def z_pass(p, second):
+        ref = chunk(p, (z + second) % 4)
+        return remote(RING + 4 + (p - 2) * 2 + second, ref, ref, z_peer(3 if second else 1))
 
     def to_twin(p):
         ref = wo.at[:, core, :, pl.ds(p * GP, GP)]
         return remote(TWIN + p - 1, ref, ref, twin)
 
-    def ring_first(p):
-        x_gather(p).wait_recv()
-        ring(p, 0).start()
-        ring(p, 1).start()
-
-    def ring_second(p):
-        ring(p, 0).wait_recv()
-        ring(p, 1).wait_recv()
-        ring(p, 2).start()
-        ring(p, 3).start()
-
-    def ring_last(p):
-        ring(p, 2).wait_recv()
-        ring(p, 3).wait_recv()
-        to_twin(p).start()
-
     for p in (2, 3, 1):
         x_gather(p).start()
+    for p in (2, 3):
+        x_gather(p, 1).start()
+
+    parts = []
+    for vector in (1.0 + scale_ref[...], shift_ref[...], gate_ref[...]):
+        rest = vector.reshape(1, D)
+        for _ in range(3):
+            part = rest.astype(BF)
+            parts.append(part)
+            rest = rest - part.astype(F32)
+    parts = jnp.concatenate(parts + [jnp.zeros((7, D), BF)], axis=0)
+    gains[...] = exact(
+        parts, spots(16, 384, lambda r: r // 3, lambda l: l // 128), (((0,), (0,)), ((), ()))
+    )
 
     def norm(f):
         rows = 32
@@ -204,7 +185,7 @@
 
         def scale(i, _):
             r = pl.ds(pl.multiple_of(i * rows, rows), rows)
-            gain, shift = gains[0, r, :], gains[1, r, :]
+            gain, shift = gains[r, 0:128], gains[r, 128:256]
             for c in range(ROWS // 128):
                 cols = slice(c * 128, (c + 1) * 128)
                 x = tok[f, r, cols].astype(F32)
@@ -239,16 +220,26 @@
         @pl.when(f == 1)
         def _():
             halo_left().start()
+            for p in (2, 3):
+                x_gather(p).wait_recv()
+                z_pass(p, 0).start()
+
+        @pl.when(f == 2)
+        def _():
+            x_gather(1).wait_recv()
+            y_ring(0).start()
+            y_ring(1).start()
 
         @pl.when(f == 3)
         def _():
             halo_right().start()
+            for p in (2, 3):
+                x_gather(p, 1).wait_recv()
+                z_pass(p, 1).start()
 
         return 0
 
     lax.fori_loop(0, FR, value, 0)
-    ring_first(2)
-    ring_first(3)
 
     load_wk.wait()
     scur[...] = jnp.zeros_like(scur)
@@ -258,25 +249,32 @@
         for h in range(NH):
             rows = slice(h * HD, (h + 1) * HD)
             fresh = exact(vbuf[2 + f, rows, :], kbuf[rows, :], NT)
-            state = decay(f, h) * scur[h] + fresh
-            scur[h] = state
+            state = decay(f, h) * scur[h, 0:HD, :] + fresh
+            scur[h, 0:HD, :] = state
             sloc[f, h] = state
+
+        @pl.when(f == 2)
+        def _():
+            y_ring(0).wait_recv()
+            y_ring(1).wait_recv()
+            y_ring(2).start()
+            y_ring(3).start()
+
         return 0
 
     lax.fori_loop(0, FR, key, 0)
 
     row_id = lax.broadcasted_iota(jnp.int32, (TT, HD), 0)
-
-    def pack(slot, h, log, state):
+    half_rows = pl.ds(pl.multiple_of(core * HALF, HALF), HALF)
+    other_rows = pl.ds(pl.multiple_of((1 - core) * HALF, HALF), HALF)
+
+    def put_log(ref, log):
         high = log.astype(BF).astype(F32)
         low = log - high
-        tail = jnp.where(row_id == 0, high, jnp.where(row_id == 1, low, 0.0))
-        pack_out[slot, h, 0:HD, :] = state.astype(BF)
-        pack_out[slot, h, HD:128, :] = tail.astype(BF)
-
-    def unpack(slot, h):
-        tail = pack_in[slot, h, HD:128, :].astype(F32)
-        return jnp.sum(tail, axis=0, keepdims=True), pack_in[slot, h, 0:HD, :].astype(F32)
+        ref[...] = jnp.where(row_id == 0, high, jnp.where(row_id == 1, low, 0.0)).astype(BF)
+
+    def get_log(ref):
+        return jnp.sum(ref[...].astype(F32), axis=0, keepdims=True)
 
     def flag(condition):
         return jnp.where(condition, 1.0, 0.0).astype(F32)
@@ -290,120 +288,161 @@
     def masked(on, pair):
         return tuple(on * a for a in pair)
 
-    def own_pair(h):
+    def own_log(h):
         log = jnp.full((1, HD), decay_ref[0, h], F32)
         for f in range(1, FR):
             log = log + jnp.full((1, HD), decay_ref[f, h], F32)
-        return log, scur[h]
+        return log
 
     first_core = flag(core == 0)
 
     def chip_pair(h):
-        own, other = own_pair(h), unpack(0, h)
+        own = own_log(h), scur[h, half_rows, :]
+        other = get_log(full_in.at[h, 128:144]), full_in[h, half_rows, :].astype(F32)
         return join(choose(first_core, own, other), choose(first_core, other, own))
 
+    def put(slot, h, pair):
+        half_out[slot, h, 0:HALF, :] = pair[1].astype(BF)
+        put_log(half_out.at[slot, h, HALF : HALF + TT], pair[0])
+
+    def get(slot, h):
+        return (
+            get_log(half_in.at[slot, h, HALF : HALF + TT]),
+            half_in[slot, h, 0:HALF, :].astype(F32),
+        )
+
     def scan_core():
-        return remote(SCAN, pack_out.at[0], pack_in.at[0], twin)
+        return remote(SCAN, full_out, full_in, twin)
 
     def scan_y(step):
-        return remote(SCAN + step, pack_out.at[1], pack_in.at[step], y_peer(step))
+        return remote(SCAN + step, half_out.at[0], half_in.at[step - 1], y_peer(step))
 
     def scan_z(step):
-        return remote(SCAN + 3 + step, pack_out.at[2], pack_in.at[3 + step], z_peer(step))
-
-    def row_prefix(h):
+        return remote(SCAN + 3 + step, half_out.at[1], half_in.at[2 + step], z_peer(step))
+
+    def scan_end():
+        return remote(SCAN + 7, end_out, end_in, twin)
+
+    def prefix(place, slot, h):
         total = None
         for step in (3, 2, 1):
-            pair = masked(flag(y >= step), unpack(step, h))
+            pair = masked(flag(place >= step), get(slot + step, h))
             total = pair if total is None else join(total, pair)
         return total
 
-    def column_prefix(h):
-        total = None
-        for step in (3, 2, 1):
-            pair = masked(flag(z >= step), unpack(3 + step, h))
-            total = pair if total is None else join(total, pair)
-        return total
-
     for h in range(NH):
-        pack(0, h, *own_pair(h))
+        full_out[h, 0:128, :] = scur[h].astype(BF)
+        put_log(full_out.at[h, 128:144], own_log(h))
     scan_core().start()
 
+    def frame_of(p):
+        return (sp + 4 - RELS[p]) % 4
+
     load_wq.wait()
 
-    def query(f, _):
-        project(2, f, qbuf.at[f])
-        return 0
-
-    ring_first(1)
+    def query(p):
+        project(2, frame_of(p), qbuf.at[frame_of(p)])
+
+    query(1)
+
     scan_core().wait_recv()
     for h in range(NH):
-        pack(1, h, *chip_pair(h))
+        put(0, h, chip_pair(h))
     for step in (1, 2, 3):
         scan_y(step).start()
 
-    lax.fori_loop(0, 2, query, 0)
-    ring_second(2)
-    ring_second(3)
+    query(2)
+    mixed_t = exact(spots(TT, TT, lambda r: r, lambda l: l), mix_ref[...], NT).astype(BF)
+    mine = exact(
+        spots(8, 128, lambda r: r + FR * tm, lambda l: l), list_ref[...].astype(BF), NT
+    )
+    mine = (mine - (FR * tm - WIN).astype(F32)).astype(BF)
+    for n in range(NBR):
+        mixrep[n] = exact(
+            mixed_t, spots(128, 128, lambda r: r, lambda l: l % TT + n * TT)
+        )
+        listed = exact(
+            mine, spots(TILES * NBR, ROWS, lambda r: r, lambda l: l // TT * NBR + n)
+        )
+        for f in range(FR):
+            rel[f, n : n + 1, :] = listed[f : f + 1]
+
+    query(3)
 
     for step in (1, 2, 3):
         scan_y(step).wait_recv()
     for h in range(NH):
-        total = join(row_prefix(h), chip_pair(h))
+        total = join(prefix(y, -1, h), chip_pair(h))
         for step in (3, 2, 1):
-            total = join(total, masked(flag(y < step), unpack(step, h)))
-        pack(2, h, *total)
+            total = join(total, masked(flag(y < step), get(step - 1, h)))
+        put(1, h, total)
     for step in (1, 2, 3):
         scan_z(step).start()
-
-    lax.fori_loop(2, FR, query, 0)
-    ring_second(1)
 
     halo_left().wait_recv()
     halo_right().wait_recv()
     tile_of_lane = lax.broadcasted_iota(jnp.int32, (TT, 128), 1) // TT
 
-    def tiles(j, _):
-        cols = pl.ds(pl.multiple_of(j * 128, 128), 128)
-        for pair in range(2):
-            for f in range(2):
-                for g in range(f, f + 2 * WIN + 1):
-                    block = jnp.zeros((TT, 128), F32)
-                    for n in range(NBR):
-                        listed = rel[n, pl.ds(2 * pair + f, 1), cols]
-                        block = block + jnp.where(listed == 2 * pair + g, mixrep[n], 0.0)
-                    for t in range(8):
-                        low = g * 128 + t * TT
-                        band[pair, low : low + TT, f * 128 : (f + 1) * 128] = jnp.where(
-                            tile_of_lane == t, block, 0.0
-                        ).astype(BF)
-            source = jnp.concatenate(
-                [vbuf[2 * pair + g, :, cols] for g in range(2 * WIN + 2)], axis=1
-            )
-            mixed = exact(source, band[pair]).astype(BF)
-            for f in range(2):
-                win[2 * pair + f, :, cols] = mixed[:, f * 128 : (f + 1) * 128]
-        return 0
-
-    lax.fori_loop(0, ROWS // 128, tiles, 0)
+    def window(p):
+        f = frame_of(p)
+
+        def tiles(j, _):
+            cols = pl.ds(pl.multiple_of(j * 128, 128), 128)
+            for g in range(2 * WIN + 1):
+                block = jnp.zeros((TT, 128), F32)
+                for n in range(NBR):
+                    listed = rel[f, n : n + 1, cols]
+                    block = block + jnp.where(listed == (f + g).astype(F32), mixrep[n], 0.0)
+                for t in range(8):
+                    low = g * 128 + t * TT
+                    band[low : low + TT, :] = jnp.where(tile_of_lane == t, block, 0.0).astype(BF)
+            source = jnp.concatenate([vbuf[f + g, :, cols] for g in range(2 * WIN + 1)], axis=1)
+            win[f, :, cols] = exact(source, band[...]).astype(BF)
+            return 0
+
+        lax.fori_loop(0, ROWS // 128, tiles, 0)
+
+    window(1)
+    window(2)
 
     for step in (1, 2, 3):
         scan_z(step).wait_recv()
     for h in range(NH):
-        chip = masked(1.0 - first_core, unpack(0, h))
-        entering = join(join(column_prefix(h), row_prefix(h)), chip)[1]
+        half = join(prefix(z, 2, h), prefix(y, -1, h))[1]
+        entry[h, half_rows, :] = half
+        end_out[h] = half.astype(BF)
+    scan_end().start()
+
+    for p in (2, 3):
+        z_pass(p, 0).wait_recv()
+        z_pass(p, 1).wait_recv()
+        to_twin(p).start()
+    y_ring(2).wait_recv()
+    y_ring(3).wait_recv()
+    to_twin(1).start()
+
+    window(3)
+
+    scan_end().wait_recv()
+    for h in range(NH):
+        entry[h, other_rows, :] = end_in[h].astype(F32)
+        before = get_log(full_in.at[h, 128:144]), full_in[h, 0:HD, :].astype(F32)
+        before = masked(1.0 - first_core, before)
+        entering = jnp.exp(before[0]) * entry[h, 0:HD, :] + before[1]
         for f in range(FR):
             entering = decay(f, h) * entering
             sloc[f, h] = sloc[f, h] + entering
 
     def swap(p):
-        f = (sp + 4 - RELS[p]) % 4
         return remote(
-            SWAP + p - 1, qbuf.at[f], mixb.at[pl.ds(p * GP, GW)], x_peer(4 - RELS[p])
+            SWAP + p - 1,
+            qbuf.at[frame_of(p)],
+            mixb.at[pl.ds(p * GP, GW)],
+            x_peer(4 - RELS[p]),
         )
 
-    for p in (1, 2, 3, 0):
-        f = (sp + 4 - RELS[p]) % 4
+    def attend(p):
+        f = frame_of(p)
         for h in range(NH):
             rows = slice(h * HD, (h + 1) * HD)
             state = jnp.zeros((HD, HD), F32)
@@ -418,14 +457,13 @@
                 mixb[rows, :] = both
             else:
                 qbuf[f, rows, :] = both
-        if p > 0:
-            swap(p).start()
-        if p == 1:
-            ring_last(2)
-        if p == 2:
-            ring_last(3)
-        if p == 3:
-            ring_last(1)
+
+    for p in (1, 2, 3):
+        attend(p)
+        swap(p).start()
+    query(0)
+    window(0)
+    attend(0)
 
     load_resid.wait()
 
@@ -441,6 +479,10 @@
     for i in range(4):
         low, high = i * 2 * PART, min((i + 1) * 2 * PART, D)
         acc[low:high, :] += exact(weights(i, 1, 1)[: high - low], mixb[GP : 2 * GP, :])
+
+    def store(i):
+        rows = pl.ds(i * 2 * PART, min(2 * PART, D - i * 2 * PART))
+        return load(9 + i, resid.at[rows], out_hbm.at[rows])
 
     for p in (2, 3):
         to_twin(p).wait_recv()
@@ -451,23 +493,28 @@
         for c in range(ROWS // 128):
             cols = slice(c * 128, (c + 1) * 128)
             resid[low:high, cols] = (
-                resid[low:high, cols].astype(F32) + gains[2, low:high, :] * total[:, cols]
+                resid[low:high, cols].astype(F32) + gains[low:high, 256:384] * total[:, cols]
             ).astype(BF)
-    store = load(9, resid, out_hbm)
-    store.start()
+        store(i).start()
 
     for p in (1, 2, 3):
         x_gather(p).wait_send()
-        for k in range(4):
-            ring(p, k).wait_send()
         to_twin(p).wait_send()
         swap(p).wait_send()
         scan_y(p).wait_send()
         scan_z(p).wait_send()
+    for p in (2, 3):
+        x_gather(p, 1).wait_send()
+        z_pass(p, 0).wait_send()
+        z_pass(p, 1).wait_send()
+    for k in range(4):
+        y_ring(k).wait_send()
     scan_core().wait_send()
+    scan_end().wait_send()
     halo_left().wait_send()
     halo_right().wait_send()
-    store.wait()
+    for i in range(4):
+        store(i).wait()
 
 
 def body(
@@ -494,15 +541,20 @@
             pltpu.VMEM((FR, GW, ROWS), BF),
             pltpu.VMEM((4 * GP, ROWS), BF),
             pltpu.VMEM((D, ROWS), F32),
-            pltpu.VMEM((3, D, 128), F32),
+            pltpu.VMEM((D, 384), F32),
             pltpu.VMEM((FR, NH, HD, HD), F32),
-            pltpu.VMEM((NH, HD, HD), F32),
-            pltpu.VMEM((3, NH, 128, HD), BF),
-            pltpu.VMEM((7, NH, 128, HD), BF),
+            pltpu.VMEM((NH, 128, HD), F32),
+            pltpu.VMEM((NH, 128, HD), F32),
+            pltpu.VMEM((NH, 144, HD), BF),
+            pltpu.VMEM((NH, 144, HD), BF),
+            pltpu.VMEM((2, NH, HALF + TT, HD), BF),
+            pltpu.VMEM((6, NH, HALF + TT, HD), BF),
+            pltpu.VMEM((NH, HALF, HD), BF),
+            pltpu.VMEM((NH, HALF, HD), BF),
             pltpu.VMEM((NBR, TT, 128), F32),
-            pltpu.VMEM((NBR, 8, ROWS), F32),
-            pltpu.VMEM((2, (2 * WIN + 2) * 128, 256), BF),
-            pltpu.SemaphoreType.DMA((10,)),
+            pltpu.VMEM((FR, NBR, ROWS), F32),
+            pltpu.VMEM(((2 * WIN + 1) * 128, 128), BF),
+            pltpu.SemaphoreType.DMA((13,)),
             pltpu.SemaphoreType.DMA((MESSAGES,)),
             pltpu.SemaphoreType.DMA((MESSAGES,)),
         ],

time: 102 us -> 99.4 us (0.975)
  Pallas kernels: 98 us -> 95.1 us
    pallas_call x1, Pallas kernels: 98 us -> 95.1 us  [body(): pl.pallas_call(kernel, out_shape=jax.ShapeDtypeStruct((D, ROWS), BF), in_...]
where the time goes in v3:
time: 99.4 us; the launch traced here: 98.2 us
  Pallas kernels  95.1 us (96%)
  local copies, waits for them, and re-layouts  3.18 us (3%)
    pallas_call x1, Pallas kernels, body(): pl.pallas_call(kernel, out_shape=jax.ShapeDtypeStruct((D, ROWS), BF), in_...  95.1 us
    unnamed x1, local copies, waits for them, and re-layouts  3.18 us

profile of v3, /device:TPU:0, one launch (start us, length us, event | category | flops | bytes accessed | tf_op | source)
XLA Modules:
  0.0 98.2 jit_solution(1932755729532256384)
XLA Ops:
  0.0 95.1 %shard_map.118 = bf16[2240,512]{1,0:T(8,128)(2,1)} custom-call(bf16[2240,2048]{1,0:T(8,128)(2,1)} %bitcast.9, f32[2240]{0:T(1024)} %scale_ref.1, f32[2240]{0:T(1024)} %shift_ref.1, f32[2240]{0:T(1024)} %gate_ref.1, bf16[560,2240]{1,0:T(8,128)(2,1)} %bitcast.11, bf16[560,2240]{1,0:T(8,128)(2,1)} %bitcast.12, bf16[560,2240]{1,0:T(8,128)(2,1)} %bitcast.13, ...), custom_call_target="tpu_custom_call" | custom-call | tf_op jit(solution)/shard_map/pallas_call | solution.py:527
  95.1 3.2 %copy.14 = bf16[512,2240]{0,1:T(8,128)(2,1)} copy(bf16[512,2240]{0,1:T(8,128)(2,1)} %bitcast.10) | data formatting | bytes 4587520

commit v4 on v3

--- a/solution.py
+++ b/solution.py
@@ -25,11 +25,12 @@
 NT = (((1,), (1,)), ((), ()))
 
 X_GATHER = 0
-RING = 5
-TWIN = 13
-HALO = 16
-SCAN = 18
-SWAP = 26
+FORWARD = 4
+Z_PASS = 6
+TWIN = 12
+HALO = 15
+SCAN = 17
+SWAP = 25
 MESSAGES = 29
 HALF = 64
 
@@ -38,7 +39,7 @@
     tok_hbm, scale_ref, shift_ref, gate_ref, wq_hbm, wk_hbm, wv_hbm, wo_hbm, mix_ref,
     decay_ref, last_ref, list_ref, out_hbm,
     tok, resid, wqkv, wo_raw, wo, vbuf, kbuf, qbuf, win, mixb, acc, gains,
-    sloc, scur, entry, full_out, full_in, half_out, half_in, end_out, end_in,
+    relay, sloc, scur, entry, full_out, full_in, half_out, half_in, end_out, end_in,
     mixrep, rel, band, local_sem, send_sem, recv_sem,
 ):
     tm = lax.axis_index("tm")
@@ -96,7 +97,7 @@
     load_resid.start()
 
     barrier = pltpu.get_barrier_semaphore()
-    partners = [x_peer(i) for i in (1, 2, 3)] + [y_peer(i) for i in (1, 2, 3)]
+    partners = [x_peer(i) for i in (1, 3)] + [y_peer(i) for i in (1, 2, 3)]
     partners += [z_peer(i) for i in (1, 2, 3)] + [twin, outer]
     for device in partners:
         pl.semaphore_signal(barrier, inc=1, device_id=device, device_id_type=MESH)
@@ -128,38 +129,38 @@
 
     pl.semaphore_wait(barrier, len(partners))
 
-    def chunk(p, i, first=0, count=PART):
-        return wo.at[i, core, pl.ds(first, count), pl.ds(p * GP, GP)]
-
-    def x_gather(p, second=0):
-        i = y if p == 1 else (z + second) % 4
-        number = X_GATHER + p - 1 + 2 * second
+    def chunk(p, i):
+        return wo.at[i, core, :, pl.ds(p * GP, GP)]
+
+    onward = x_peer(1 + 2 * core)
+
+    def x_gather(p, second):
+        i = (z + second) % 4
+        number = X_GATHER + (p - 2) * 2 + second
         return remote(number, chunk(0, i), chunk(p, i), x_peer(4 - RELS[p]))
 
-    def y_ring(k):
-        below, above = (y + 3) % 4, (y + 1) % 4
-        if k == 0:
-            ref, device = chunk(1, y), y_peer(1)
-        elif k == 1:
-            ref, device = chunk(1, y), y_peer(3)
-        elif k == 2:
-            ref, device = chunk(1, below, 0, PART // 2), y_peer(1)
-        else:
-            ref, device = chunk(1, above, PART // 2, PART // 2), y_peer(3)
-        return remote(RING + k, ref, ref, device)
+    def x_forward(second):
+        i = (z + second) % 4
+        cols = pl.ds(pl.multiple_of((2 + core) * GP, 128), GP)
+        return remote(FORWARD + second, wo.at[i, core, :, cols], chunk(1, i), onward)
 
     def z_pass(p, second):
         ref = chunk(p, (z + second) % 4)
-        return remote(RING + 4 + (p - 2) * 2 + second, ref, ref, z_peer(3 if second else 1))
+        return remote(Z_PASS + (p - 1) * 2 + second, ref, ref, z_peer(3 if second else 1))
+
+    def x_arrived(second):
+        for p in (2, 3):
+            x_gather(p, second).wait_recv()
+            z_pass(p, second).start()
+        x_forward(second).start()
 
     def to_twin(p):
         ref = wo.at[:, core, :, pl.ds(p * GP, GP)]
         return remote(TWIN + p - 1, ref, ref, twin)
 
-    for p in (2, 3, 1):
-        x_gather(p).start()
-    for p in (2, 3):
-        x_gather(p, 1).start()
+    for second in (0, 1):
+        for p in (2, 3):
+            x_gather(p, second).start()
 
     parts = []
     for vector in (1.0 + scale_ref[...], shift_ref[...], gate_ref[...]):
@@ -220,22 +221,14 @@
         @pl.when(f == 1)
         def _():
             halo_left().start()
-            for p in (2, 3):
-                x_gather(p).wait_recv()
-                z_pass(p, 0).start()
 
         @pl.when(f == 2)
         def _():
-            x_gather(1).wait_recv()
-            y_ring(0).start()
-            y_ring(1).start()
+            x_arrived(0)
 
         @pl.when(f == 3)
         def _():
             halo_right().start()
-            for p in (2, 3):
-                x_gather(p, 1).wait_recv()
-                z_pass(p, 1).start()
 
         return 0
 
@@ -253,12 +246,9 @@
             scur[h, 0:HD, :] = state
             sloc[f, h] = state
 
-        @pl.when(f == 2)
+        @pl.when(f == 1)
         def _():
-            y_ring(0).wait_recv()
-            y_ring(1).wait_recv()
-            y_ring(2).start()
-            y_ring(3).start()
+            x_arrived(1)
 
         return 0
 
@@ -413,13 +403,13 @@
         end_out[h] = half.astype(BF)
     scan_end().start()
 
+    for second in (0, 1):
+        x_forward(second).wait_recv()
+        z_pass(1, second).start()
     for p in (2, 3):
         z_pass(p, 0).wait_recv()
         z_pass(p, 1).wait_recv()
         to_twin(p).start()
-    y_ring(2).wait_recv()
-    y_ring(3).wait_recv()
-    to_twin(1).start()
 
     window(3)
 
@@ -434,12 +424,13 @@
             sloc[f, h] = sloc[f, h] + entering
 
     def swap(p):
-        return remote(
-            SWAP + p - 1,
-            qbuf.at[frame_of(p)],
-            mixb.at[pl.ds(p * GP, GW)],
-            x_peer(4 - RELS[p]),
-        )
+        mixed = qbuf.at[frame_of(p)]
+        if p == 1:
+            return remote(SWAP + 2, mixed, relay, onward)
+        return remote(SWAP + p - 2, mixed, mixb.at[pl.ds(p * GP, GW)], x_peer(4 - RELS[p]))
+
+    def swap_onward():
+        return remote(SWAP + 3, relay, mixb.at[pl.ds(GP, GW)], onward)
 
     def attend(p):
         f = frame_of(p)
@@ -464,6 +455,11 @@
     query(0)
     window(0)
     attend(0)
+    swap(1).wait_recv()
+    swap_onward().start()
+    z_pass(1, 0).wait_recv()
+    z_pass(1, 1).wait_recv()
+    to_twin(1).start()
 
     load_resid.wait()
 
@@ -473,23 +469,23 @@
     for i in range(4):
         low, high = i * 2 * PART, min((i + 1) * 2 * PART, D)
         acc[low:high, :] = exact(weights(i, 0, 1)[: high - low], mixb[0:GP, :])
-
-    to_twin(1).wait_recv()
-    swap(1).wait_recv()
-    for i in range(4):
-        low, high = i * 2 * PART, min((i + 1) * 2 * PART, D)
-        acc[low:high, :] += exact(weights(i, 1, 1)[: high - low], mixb[GP : 2 * GP, :])
-
-    def store(i):
-        rows = pl.ds(i * 2 * PART, min(2 * PART, D - i * 2 * PART))
-        return load(9 + i, resid.at[rows], out_hbm.at[rows])
 
     for p in (2, 3):
         to_twin(p).wait_recv()
         swap(p).wait_recv()
     for i in range(4):
         low, high = i * 2 * PART, min((i + 1) * 2 * PART, D)
-        total = acc[low:high, :] + exact(weights(i, 2, 2)[: high - low], mixb[2 * GP : 4 * GP, :])
+        acc[low:high, :] += exact(weights(i, 2, 2)[: high - low], mixb[2 * GP : 4 * GP, :])
+
+    def store(i):
+        rows = pl.ds(i * 2 * PART, min(2 * PART, D - i * 2 * PART))
+        return load(9 + i, resid.at[rows], out_hbm.at[rows])
+
+    to_twin(1).wait_recv()
+    swap_onward().wait_recv()
+    for i in range(4):
+        low, high = i * 2 * PART, min((i + 1) * 2 * PART, D)
+        total = acc[low:high, :] + exact(weights(i, 1, 1)[: high - low], mixb[GP : 2 * GP, :])
         for c in range(ROWS // 128):
             cols = slice(c * 128, (c + 1) * 128)
             resid[low:high, cols] = (
@@ -498,17 +494,17 @@
         store(i).start()
 
     for p in (1, 2, 3):
-        x_gather(p).wait_send()
         to_twin(p).wait_send()
         swap(p).wait_send()
         scan_y(p).wait_send()
         scan_z(p).wait_send()
-    for p in (2, 3):
-        x_gather(p, 1).wait_send()
-        z_pass(p, 0).wait_send()
-        z_pass(p, 1).wait_send()
-    for k in range(4):
-        y_ring(k).wait_send()
+    for second in (0, 1):
+        for p in (1, 2, 3):
+            z_pass(p, second).wait_send()
+            if p > 1:
+                x_gather(p, second).wait_send()
+        x_forward(second).wait_send()
+    swap_onward().wait_send()
     scan_core().wait_send()
     scan_end().wait_send()
     halo_left().wait_send()
@@ -542,6 +538,7 @@
             pltpu.VMEM((4 * GP, ROWS), BF),
             pltpu.VMEM((D, ROWS), F32),
             pltpu.VMEM((D, 384), F32),
+            pltpu.VMEM((GW, ROWS), BF),
             pltpu.VMEM((FR, NH, HD, HD), F32),
             pltpu.VMEM((NH, 128, HD), F32),
             pltpu.VMEM((NH, 128, HD), F32),

time: 99.4 us -> 89.9 us (0.904); the launches traced: 98.2 us -> 89.8 us
  Pallas kernels: 95.1 us -> 86.6 us
    pallas_call x1, Pallas kernels: 95.1 us -> 86.6 us  [body(): pl.pallas_call(kernel, out_shape=jax.ShapeDtypeStruct((D, ROWS), BF), in_...]
where the time goes in v4:
time: 89.9 us; the launch traced here: 89.8 us
  Pallas kernels  86.6 us (96%)
  local copies, waits for them, and re-layouts  3.18 us (4%)
    pallas_call x1, Pallas kernels, body(): pl.pallas_call(kernel, out_shape=jax.ShapeDtypeStruct((D, ROWS), BF), in_...  86.6 us
    unnamed x1, local copies, waits for them, and re-layouts  3.18 us

profile of v4, /device:TPU:0, one launch (start us, length us, event | category | flops | bytes accessed | tf_op | source)
XLA Modules:
  0.0 89.8 jit_solution(17307037334105318252)
XLA Ops:
  0.0 86.6 %shard_map.118 = bf16[2240,512]{1,0:T(8,128)(2,1)} custom-call(bf16[2240,2048]{1,0:T(8,128)(2,1)} %bitcast.9, f32[2240]{0:T(1024)} %scale_ref.1, f32[2240]{0:T(1024)} %shift_ref.1, f32[2240]{0:T(1024)} %gate_ref.1, bf16[560,2240]{1,0:T(8,128)(2,1)} %bitcast.11, bf16[560,2240]{1,0:T(8,128)(2,1)} %bitcast.12, bf16[560,2240]{1,0:T(8,128)(2,1)} %bitcast.13, ...), custom_call_target="tpu_custom_call" | custom-call | tf_op jit(solution)/shard_map/pallas_call | solution.py:523
  86.6 3.2 %copy.14 = bf16[512,2240]{0,1:T(8,128)(2,1)} copy(bf16[512,2240]{0,1:T(8,128)(2,1)} %bitcast.10) | data formatting | bytes 4587520

commit v5 on v4

--- a/solution.py
+++ b/solution.py
@@ -26,7 +26,7 @@
 
 X_GATHER = 0
 FORWARD = 4
-Z_PASS = 6
+SIDE_PASS = 6
 TWIN = 12
 HALO = 15
 SCAN = 17
@@ -134,24 +134,34 @@
 
     onward = x_peer(1 + 2 * core)
 
+    def place(p):
+        if p == 2:
+            return z, z_peer
+        if p == 3:
+            return y, y_peer
+        return z + core * (y - z), lambda step: at(
+            (z + (1 - core) * step) % 4, (y + core * step) % 4, core
+        )
+
     def x_gather(p, second):
-        i = (z + second) % 4
+        i = (place(p)[0] + second) % 4
         number = X_GATHER + (p - 2) * 2 + second
         return remote(number, chunk(0, i), chunk(p, i), x_peer(4 - RELS[p]))
 
     def x_forward(second):
-        i = (z + second) % 4
+        i = (place(1)[0] + second) % 4
         cols = pl.ds(pl.multiple_of((2 + core) * GP, 128), GP)
         return remote(FORWARD + second, wo.at[i, core, :, cols], chunk(1, i), onward)
 
-    def z_pass(p, second):
-        ref = chunk(p, (z + second) % 4)
-        return remote(Z_PASS + (p - 1) * 2 + second, ref, ref, z_peer(3 if second else 1))
+    def side_pass(p, second):
+        i, peer = place(p)
+        ref = chunk(p, (i + second) % 4)
+        return remote(SIDE_PASS + (p - 1) * 2 + second, ref, ref, peer(3 if second else 1))
 
     def x_arrived(second):
         for p in (2, 3):
             x_gather(p, second).wait_recv()
-            z_pass(p, second).start()
+            side_pass(p, second).start()
         x_forward(second).start()
 
     def to_twin(p):
@@ -211,6 +221,14 @@
                 wqkv[weight], tok[f, :, cols], preferred_element_type=F32
             ).astype(BF)
 
+    @pl.when(tm == 0)
+    def _():
+        vbuf[0:2] = jnp.zeros((2, GW, ROWS), BF)
+
+    @pl.when(tm == 31)
+    def _():
+        vbuf[6:8] = jnp.zeros((2, GW, ROWS), BF)
+
     load_wv.wait()
 
     def value(f, _):
@@ -220,7 +238,9 @@
 
         @pl.when(f == 1)
         def _():
-            halo_left().start()
+            @pl.when(tm > 0)
+            def _():
+                halo_left().start()
 
         @pl.when(f == 2)
         def _():
@@ -228,7 +248,9 @@
 
         @pl.when(f == 3)
         def _():
-            halo_right().start()
+            @pl.when(tm < 31)
+            def _():
+                halo_right().start()
 
         return 0
 
@@ -291,15 +313,19 @@
         other = get_log(full_in.at[h, 128:144]), full_in[h, half_rows, :].astype(F32)
         return join(choose(first_core, own, other), choose(first_core, other, own))
 
-    def put(slot, h, pair):
-        half_out[slot, h, 0:HALF, :] = pair[1].astype(BF)
-        put_log(half_out.at[slot, h, HALF : HALF + TT], pair[0])
+    def put(slot, pairs):
+        logs = jnp.zeros((TT, HD), F32)
+        for h, (log, state) in enumerate(pairs):
+            half_out[slot, h * HALF : (h + 1) * HALF, :] = state.astype(BF)
+            high = log.astype(BF).astype(F32)
+            logs = jnp.where(row_id == 2 * h, high, logs)
+            logs = jnp.where(row_id == 2 * h + 1, log - high, logs)
+        half_out[slot, NH * HALF :, :] = logs.astype(BF)
 
     def get(slot, h):
-        return (
-            get_log(half_in.at[slot, h, HALF : HALF + TT]),
-            half_in[slot, h, 0:HALF, :].astype(F32),
-        )
+        logs = half_in[slot, NH * HALF :, :].astype(F32)
+        log = jnp.sum(jnp.where(row_id // 2 == h, logs, 0.0), axis=0, keepdims=True)
+        return log, half_in[slot, h * HALF : (h + 1) * HALF, :].astype(F32)
 
     def scan_core():
         return remote(SCAN, full_out, full_in, twin)
@@ -336,8 +362,7 @@
     query(1)
 
     scan_core().wait_recv()
-    for h in range(NH):
-        put(0, h, chip_pair(h))
+    put(0, [chip_pair(h) for h in range(NH)])
     for step in (1, 2, 3):
         scan_y(step).start()
 
@@ -358,19 +383,28 @@
             rel[f, n : n + 1, :] = listed[f : f + 1]
 
     query(3)
+    query(0)
 
     for step in (1, 2, 3):
         scan_y(step).wait_recv()
+    totals = []
     for h in range(NH):
         total = join(prefix(y, -1, h), chip_pair(h))
         for step in (3, 2, 1):
             total = join(total, masked(flag(y < step), get(step - 1, h)))
-        put(1, h, total)
+        totals.append(total)
+    put(1, totals)
     for step in (1, 2, 3):
         scan_z(step).start()
 
-    halo_left().wait_recv()
-    halo_right().wait_recv()
+    @pl.when(tm < 31)
+    def _():
+        halo_left().wait_recv()
+
+    @pl.when(tm > 0)
+    def _():
+        halo_right().wait_recv()
+
     tile_of_lane = lax.broadcasted_iota(jnp.int32, (TT, 128), 1) // TT
 
     def window(p):
@@ -394,6 +428,7 @@
 
     window(1)
     window(2)
+    window(3)
 
     for step in (1, 2, 3):
         scan_z(step).wait_recv()
@@ -405,13 +440,13 @@
 
     for second in (0, 1):
         x_forward(second).wait_recv()
-        z_pass(1, second).start()
+        side_pass(1, second).start()
     for p in (2, 3):
-        z_pass(p, 0).wait_recv()
-        z_pass(p, 1).wait_recv()
+        side_pass(p, 0).wait_recv()
+        side_pass(p, 1).wait_recv()
         to_twin(p).start()
 
-    window(3)
+    window(0)
 
     scan_end().wait_recv()
     for h in range(NH):
@@ -452,13 +487,11 @@
     for p in (1, 2, 3):
         attend(p)
         swap(p).start()
-    query(0)
-    window(0)
     attend(0)
     swap(1).wait_recv()
     swap_onward().start()
-    z_pass(1, 0).wait_recv()
-    z_pass(1, 1).wait_recv()
+    side_pass(1, 0).wait_recv()
+    side_pass(1, 1).wait_recv()
     to_twin(1).start()
 
     load_resid.wait()
@@ -500,15 +533,22 @@
         scan_z(p).wait_send()
     for second in (0, 1):
         for p in (1, 2, 3):
-            z_pass(p, second).wait_send()
+            side_pass(p, second).wait_send()
             if p > 1:
                 x_gather(p, second).wait_send()
         x_forward(second).wait_send()
     swap_onward().wait_send()
     scan_core().wait_send()
     scan_end().wait_send()
-    halo_left().wait_send()
-    halo_right().wait_send()
+
+    @pl.when(tm > 0)
+    def _():
+        halo_left().wait_send()
+
+    @pl.when(tm < 31)
+    def _():
+        halo_right().wait_send()
+
     for i in range(4):
         store(i).wait()
 
@@ -544,8 +584,8 @@
             pltpu.VMEM((NH, 128, HD), F32),
             pltpu.VMEM((NH, 144, HD), BF),
             pltpu.VMEM((NH, 144, HD), BF),
-            pltpu.VMEM((2, NH, HALF + TT, HD), BF),
-            pltpu.VMEM((6, NH, HALF + TT, HD), BF),
+            pltpu.VMEM((2, NH * HALF + TT, HD), BF),
+            pltpu.VMEM((6, NH * HALF + TT, HD), BF),
             pltpu.VMEM((NH, HALF, HD), BF),
             pltpu.VMEM((NH, HALF, HD), BF),
             pltpu.VMEM((NBR, TT, 128), F32),

time: 89.9 us -> 86.2 us (0.959)
  Pallas kernels: 86.6 us -> 82.6 us
    pallas_call x1, Pallas kernels: 86.6 us -> 82.6 us  [body(): pl.pallas_call(kernel, out_shape=jax.ShapeDtypeStruct((D, ROWS), BF), in_...]
where the time goes in v5:
time: 86.2 us; the launch traced here: 85.8 us
  Pallas kernels  82.6 us (96%)
  local copies, waits for them, and re-layouts  3.18 us (4%)
    pallas_call x1, Pallas kernels, body(): pl.pallas_call(kernel, out_shape=jax.ShapeDtypeStruct((D, ROWS), BF), in_...  82.6 us
    unnamed x1, local copies, waits for them, and re-layouts  3.18 us

profile of v5, /device:TPU:0, one launch (start us, length us, event | category | flops | bytes accessed | tf_op | source)
XLA Modules:
  0.0 85.8 jit_solution(19420894393588044)
XLA Ops:
  0.0 82.6 %shard_map.118 = bf16[2240,512]{1,0:T(8,128)(2,1)} custom-call(bf16[2240,2048]{1,0:T(8,128)(2,1)} %bitcast.9, f32[2240]{0:T(1024)} %scale_ref.1, f32[2240]{0:T(1024)} %shift_ref.1, f32[2240]{0:T(1024)} %gate_ref.1, bf16[560,2240]{1,0:T(8,128)(2,1)} %bitcast.11, bf16[560,2240]{1,0:T(8,128)(2,1)} %bitcast.12, bf16[560,2240]{1,0:T(8,128)(2,1)} %bitcast.13, ...), custom_call_target="tpu_custom_call" | custom-call | tf_op jit(solution)/shard_map/pallas_call | solution.py:563
  82.6 3.2 %copy.14 = bf16[512,2240]{0,1:T(8,128)(2,1)} copy(bf16[512,2240]{0,1:T(8,128)(2,1)} %bitcast.10) | data formatting | bytes 4587520

commit v6 on v5

--- a/solution.py
+++ b/solution.py
@@ -31,7 +31,8 @@
 HALO = 15
 SCAN = 17
 SWAP = 25
-MESSAGES = 29
+FAR = 29
+MESSAGES = 35
 HALF = 64
 
 
@@ -39,7 +40,7 @@
     tok_hbm, scale_ref, shift_ref, gate_ref, wq_hbm, wk_hbm, wv_hbm, wo_hbm, mix_ref,
     decay_ref, last_ref, list_ref, out_hbm,
     tok, resid, wqkv, wo_raw, wo, vbuf, kbuf, qbuf, win, mixb, acc, gains,
-    relay, sloc, scur, entry, full_out, full_in, half_out, half_in, end_out, end_in,
+    relay, distant, states_out, states_relay, states_in, sloc, scur, entry, full_out, full_in, half_out, half_in, end_out, end_in,
     mixrep, rel, band, local_sem, send_sem, recv_sem,
 ):
     tm = lax.axis_index("tm")
@@ -359,7 +360,17 @@
     def query(p):
         project(2, frame_of(p), qbuf.at[frame_of(p)])
 
+    def far(kind, leg):
+        if kind == 0:
+            refs = qbuf.at[frame_of(1)], relay.at[0], distant.at[0]
+        elif kind == 1:
+            refs = win.at[frame_of(1)], relay.at[1], distant.at[1]
+        else:
+            refs = states_out, states_relay, states_in
+        return remote(FAR + kind * 2 + leg, refs[leg], refs[leg + 1], onward)
+
     query(1)
+    far(0, 0).start()
 
     scan_core().wait_recv()
     put(0, [chip_pair(h) for h in range(NH)])
@@ -383,19 +394,8 @@
             rel[f, n : n + 1, :] = listed[f : f + 1]
 
     query(3)
-    query(0)
-
-    for step in (1, 2, 3):
-        scan_y(step).wait_recv()
-    totals = []
-    for h in range(NH):
-        total = join(prefix(y, -1, h), chip_pair(h))
-        for step in (3, 2, 1):
-            total = join(total, masked(flag(y < step), get(step - 1, h)))
-        totals.append(total)
-    put(1, totals)
-    for step in (1, 2, 3):
-        scan_z(step).start()
+    far(0, 0).wait_recv()
+    far(0, 1).start()
 
     @pl.when(tm < 31)
     def _():
@@ -427,8 +427,25 @@
         lax.fori_loop(0, ROWS // 128, tiles, 0)
 
     window(1)
+    far(1, 0).start()
+
+    for step in (1, 2, 3):
+        scan_y(step).wait_recv()
+    totals = []
+    for h in range(NH):
+        total = join(prefix(y, -1, h), chip_pair(h))
+        for step in (3, 2, 1):
+            total = join(total, masked(flag(y < step), get(step - 1, h)))
+        totals.append(total)
+    put(1, totals)
+    for step in (1, 2, 3):
+        scan_z(step).start()
+
     window(2)
+    query(0)
     window(3)
+    far(1, 0).wait_recv()
+    far(1, 1).start()
 
     for step in (1, 2, 3):
         scan_z(step).wait_recv()
@@ -458,38 +475,43 @@
             entering = decay(f, h) * entering
             sloc[f, h] = sloc[f, h] + entering
 
-    def swap(p):
-        mixed = qbuf.at[frame_of(p)]
-        if p == 1:
-            return remote(SWAP + 2, mixed, relay, onward)
-        return remote(SWAP + p - 2, mixed, mixb.at[pl.ds(p * GP, GW)], x_peer(4 - RELS[p]))
-
-    def swap_onward():
-        return remote(SWAP + 3, relay, mixb.at[pl.ds(GP, GW)], onward)
-
-    def attend(p):
-        f = frame_of(p)
-        for h in range(NH):
-            rows = slice(h * HD, (h + 1) * HD)
-            state = jnp.zeros((HD, HD), F32)
-            for g in range(FR):
-                state = state + flag(last_ref[f] == FR * tm + g) * sloc[g, h]
-            linear = exact(state.astype(BF), qbuf[f, rows, :])
-            inverse = lax.rsqrt(
-                jnp.sum(linear * linear, axis=0, keepdims=True) * (1.0 / HD) + EPS
-            )
-            both = (linear * inverse + win[f, rows, :].astype(F32)).astype(BF)
-            if p == 0:
-                mixb[rows, :] = both
-            else:
-                qbuf[f, rows, :] = both
-
-    for p in (1, 2, 3):
-        attend(p)
-        swap(p).start()
-    attend(0)
-    swap(1).wait_recv()
-    swap_onward().start()
+    def state_of(p, h):
+        state = jnp.zeros((HD, HD), F32)
+        for g in range(FR):
+            state = state + flag(last_ref[frame_of(p)] == FR * tm + g) * sloc[g, h]
+        return state.astype(BF)
+
+    def attend(state, query_ref, window_ref, out_ref, h, cols):
+        rows = slice(h * HD, (h + 1) * HD)
+        linear = exact(state, query_ref[rows, cols])
+        inverse = lax.rsqrt(jnp.sum(linear * linear, axis=0, keepdims=True) * (1.0 / HD) + EPS)
+        out_ref[rows, cols] = (linear * inverse + window_ref[rows, cols].astype(F32)).astype(BF)
+
+    def half_cols(half):
+        return pl.ds(half * 256, 256)
+
+    def swap(p, half):
+        return remote(
+            SWAP + (p - 2) * 2 + half,
+            qbuf.at[frame_of(p), :, half_cols(half)],
+            mixb.at[pl.ds(p * GP, GW), half_cols(half)],
+            x_peer(4 - RELS[p]),
+        )
+
+    for h in range(NH):
+        states_out[h] = state_of(1, h)
+    far(2, 0).start()
+    for half in range(2):
+        for p in (2, 3):
+            f = frame_of(p)
+            for h in range(NH):
+                attend(state_of(p, h), qbuf.at[f], win.at[f], qbuf.at[f], h, half_cols(half))
+            swap(p, half).start()
+    far(2, 0).wait_recv()
+    far(2, 1).start()
+    for h in range(NH):
+        f = frame_of(0)
+        attend(state_of(0, h), qbuf.at[f], win.at[f], mixb.at[pl.ds(0, GW)], h, slice(0, ROWS))
     side_pass(1, 0).wait_recv()
     side_pass(1, 1).wait_recv()
     to_twin(1).start()
@@ -503,32 +525,43 @@
         low, high = i * 2 * PART, min((i + 1) * 2 * PART, D)
         acc[low:high, :] = exact(weights(i, 0, 1)[: high - low], mixb[0:GP, :])
 
+    for kind in range(3):
+        far(kind, 1).wait_recv()
+    for h in range(NH):
+        attend(
+            states_in[h], distant.at[0], distant.at[1], mixb.at[pl.ds(GP, GW)], h, slice(0, ROWS)
+        )
+    to_twin(1).wait_recv()
+    for i in range(4):
+        low, high = i * 2 * PART, min((i + 1) * 2 * PART, D)
+        acc[low:high, :] += exact(weights(i, 1, 1)[: high - low], mixb[GP : 2 * GP, :])
+
+    def store(i, half):
+        rows = pl.ds(i * 2 * PART, min(2 * PART, D - i * 2 * PART))
+        cols = half_cols(half)
+        return load(9 + i + 4 * half, resid.at[rows, cols], out_hbm.at[rows, cols])
+
     for p in (2, 3):
         to_twin(p).wait_recv()
-        swap(p).wait_recv()
-    for i in range(4):
-        low, high = i * 2 * PART, min((i + 1) * 2 * PART, D)
-        acc[low:high, :] += exact(weights(i, 2, 2)[: high - low], mixb[2 * GP : 4 * GP, :])
-
-    def store(i):
-        rows = pl.ds(i * 2 * PART, min(2 * PART, D - i * 2 * PART))
-        return load(9 + i, resid.at[rows], out_hbm.at[rows])
-
-    to_twin(1).wait_recv()
-    swap_onward().wait_recv()
-    for i in range(4):
-        low, high = i * 2 * PART, min((i + 1) * 2 * PART, D)
-        total = acc[low:high, :] + exact(weights(i, 1, 1)[: high - low], mixb[GP : 2 * GP, :])
-        for c in range(ROWS // 128):
-            cols = slice(c * 128, (c + 1) * 128)
-            resid[low:high, cols] = (
-                resid[low:high, cols].astype(F32) + gains[low:high, 256:384] * total[:, cols]
-            ).astype(BF)
-        store(i).start()
+    for half in range(2):
+        for p in (2, 3):
+            swap(p, half).wait_recv()
+        near = slice(half * 256, (half + 1) * 256)
+        for i in range(4):
+            low, high = i * 2 * PART, min((i + 1) * 2 * PART, D)
+            total = acc[low:high, near] + exact(
+                weights(i, 2, 2)[: high - low], mixb[2 * GP : 4 * GP, near]
+            )
+            for c in range(2):
+                cols = slice(half * 256 + c * 128, half * 256 + (c + 1) * 128)
+                resid[low:high, cols] = (
+                    resid[low:high, cols].astype(F32)
+                    + gains[low:high, 256:384] * total[:, c * 128 : (c + 1) * 128]
+                ).astype(BF)
+            store(i, half).start()
 
     for p in (1, 2, 3):
         to_twin(p).wait_send()
-        swap(p).wait_send()
         scan_y(p).wait_send()
         scan_z(p).wait_send()
     for second in (0, 1):
@@ -537,7 +570,12 @@
             if p > 1:
                 x_gather(p, second).wait_send()
         x_forward(second).wait_send()
-    swap_onward().wait_send()
+    for half in range(2):
+        for p in (2, 3):
+            swap(p, half).wait_send()
+    for kind in range(3):
+        for leg in range(2):
+            far(kind, leg).wait_send()
     scan_core().wait_send()
     scan_end().wait_send()
 
@@ -549,8 +587,9 @@
     def _():
         halo_right().wait_send()
 
-    for i in range(4):
-        store(i).wait()
+    for half in range(2):
+        for i in range(4):
+            store(i, half).wait()
 
 
 def body(
@@ -578,7 +617,11 @@
             pltpu.VMEM((4 * GP, ROWS), BF),
             pltpu.VMEM((D, ROWS), F32),
             pltpu.VMEM((D, 384), F32),
-            pltpu.VMEM((GW, ROWS), BF),
+            pltpu.VMEM((2, GW, ROWS), BF),
+            pltpu.VMEM((2, GW, ROWS), BF),
+            pltpu.VMEM((NH, HD, HD), BF),
+            pltpu.VMEM((NH, HD, HD), BF),
+            pltpu.VMEM((NH, HD, HD), BF),
             pltpu.VMEM((FR, NH, HD, HD), F32),
             pltpu.VMEM((NH, 128, HD), F32),
             pltpu.VMEM((NH, 128, HD), F32),
@@ -591,7 +634,7 @@
             pltpu.VMEM((NBR, TT, 128), F32),
             pltpu.VMEM((FR, NBR, ROWS), F32),
             pltpu.VMEM(((2 * WIN + 1) * 128, 128), BF),
-            pltpu.SemaphoreType.DMA((13,)),
+            pltpu.SemaphoreType.DMA((17,)),
             pltpu.SemaphoreType.DMA((MESSAGES,)),
             pltpu.SemaphoreType.DMA((MESSAGES,)),
         ],

time: 86.2 us -> 93 us (1.079)
  Pallas kernels: 82.6 us -> 89.6 us
    pallas_call x1, Pallas kernels: 82.6 us -> 89.6 us  [body(): pl.pallas_call(kernel, out_shape=jax.ShapeDtypeStruct((D, ROWS), BF), in_...]
where the time goes in v6:
time: 93 us; the launch traced here: 92.8 us
  Pallas kernels  89.6 us (96%)
  local copies, waits for them, and re-layouts  3.18 us (3%)
    pallas_call x1, Pallas kernels, body(): pl.pallas_call(kernel, out_shape=jax.ShapeDtypeStruct((D, ROWS), BF), in_...  89.6 us
    unnamed x1, local copies, waits for them, and re-layouts  3.18 us

profile of v6, /device:TPU:0, one launch (start us, length us, event | category | flops | bytes accessed | tf_op | source)
XLA Modules:
  0.0 92.8 jit_solution(10430837866246988808)
XLA Ops:
  0.0 89.6 %shard_map.118 = bf16[2240,512]{1,0:T(8,128)(2,1)} custom-call(bf16[2240,2048]{1,0:T(8,128)(2,1)} %bitcast.9, f32[2240]{0:T(1024)} %scale_ref.1, f32[2240]{0:T(1024)} %shift_ref.1, f32[2240]{0:T(1024)} %gate_ref.1, bf16[560,2240]{1,0:T(8,128)(2,1)} %bitcast.11, bf16[560,2240]{1,0:T(8,128)(2,1)} %bitcast.12, bf16[560,2240]{1,0:T(8,128)(2,1)} %bitcast.13, ...), custom_call_target="tpu_custom_call" | custom-call | tf_op jit(solution)/shard_map/pallas_call | solution.py:602
  89.7 3.2 %copy.14 = bf16[512,2240]{0,1:T(8,128)(2,1)} copy(bf16[512,2240]{0,1:T(8,128)(2,1)} %bitcast.10) | data formatting | bytes 4587520

commit v7 on v5

--- a/solution.py
+++ b/solution.py
@@ -31,7 +31,7 @@
 HALO = 15
 SCAN = 17
 SWAP = 25
-MESSAGES = 29
+MESSAGES = 31
 HALF = 64
 
 
@@ -215,11 +215,7 @@
         return jnp.exp(jnp.full((1, HD), decay_ref[f, h], F32))
 
     def project(weight, f, dst):
-        for half in range(2):
-            cols = slice(half * 256, (half + 1) * 256)
-            dst[:, cols] = jnp.dot(
-                wqkv[weight], tok[f, :, cols], preferred_element_type=F32
-            ).astype(BF)
+        dst[...] = exact(wqkv[weight], tok[f]).astype(BF)
 
     @pl.when(tm == 0)
     def _():
@@ -268,7 +264,7 @@
             scur[h, 0:HD, :] = state
             sloc[f, h] = state
 
-        @pl.when(f == 1)
+        @pl.when(f == 3)
         def _():
             x_arrived(1)
 
@@ -459,37 +455,47 @@
             sloc[f, h] = sloc[f, h] + entering
 
     def swap(p):
-        mixed = qbuf.at[frame_of(p)]
-        if p == 1:
-            return remote(SWAP + 2, mixed, relay, onward)
-        return remote(SWAP + p - 2, mixed, mixb.at[pl.ds(p * GP, GW)], x_peer(4 - RELS[p]))
-
-    def swap_onward():
-        return remote(SWAP + 3, relay, mixb.at[pl.ds(GP, GW)], onward)
-
-    def attend(p):
+        return remote(
+            SWAP + p - 2,
+            qbuf.at[frame_of(p)],
+            mixb.at[pl.ds(p * GP, GW)],
+            x_peer(4 - RELS[p]),
+        )
+
+    def far(leg, half):
+        cols = pl.ds(half * 256, 256)
+        refs = qbuf.at[frame_of(1), :, cols], relay.at[:, cols], mixb.at[pl.ds(GP, GW), cols]
+        return remote(SWAP + 2 + leg * 2 + half, refs[leg], refs[leg + 1], onward)
+
+    def attend(p, low=0, high=ROWS):
         f = frame_of(p)
+        cols = slice(low, high)
         for h in range(NH):
             rows = slice(h * HD, (h + 1) * HD)
             state = jnp.zeros((HD, HD), F32)
             for g in range(FR):
                 state = state + flag(last_ref[f] == FR * tm + g) * sloc[g, h]
-            linear = exact(state.astype(BF), qbuf[f, rows, :])
+            linear = exact(state.astype(BF), qbuf[f, rows, cols])
             inverse = lax.rsqrt(
                 jnp.sum(linear * linear, axis=0, keepdims=True) * (1.0 / HD) + EPS
             )
-            both = (linear * inverse + win[f, rows, :].astype(F32)).astype(BF)
+            both = (linear * inverse + win[f, rows, cols].astype(F32)).astype(BF)
             if p == 0:
-                mixb[rows, :] = both
+                mixb[rows, cols] = both
             else:
-                qbuf[f, rows, :] = both
-
-    for p in (1, 2, 3):
+                qbuf[f, rows, cols] = both
+
+    for half in range(2):
+        attend(1, half * 256, (half + 1) * 256)
+        far(0, half).start()
+    for p in (2, 3):
         attend(p)
         swap(p).start()
+    far(0, 0).wait_recv()
+    far(1, 0).start()
     attend(0)
-    swap(1).wait_recv()
-    swap_onward().start()
+    far(0, 1).wait_recv()
+    far(1, 1).start()
     side_pass(1, 0).wait_recv()
     side_pass(1, 1).wait_recv()
     to_twin(1).start()
@@ -510,25 +516,32 @@
         low, high = i * 2 * PART, min((i + 1) * 2 * PART, D)
         acc[low:high, :] += exact(weights(i, 2, 2)[: high - low], mixb[2 * GP : 4 * GP, :])
 
-    def store(i):
+    def store(i, half):
         rows = pl.ds(i * 2 * PART, min(2 * PART, D - i * 2 * PART))
-        return load(9 + i, resid.at[rows], out_hbm.at[rows])
+        cols = pl.ds(half * 256, 256)
+        return load(9 + i + 4 * half, resid.at[rows, cols], out_hbm.at[rows, cols])
 
     to_twin(1).wait_recv()
-    swap_onward().wait_recv()
-    for i in range(4):
-        low, high = i * 2 * PART, min((i + 1) * 2 * PART, D)
-        total = acc[low:high, :] + exact(weights(i, 1, 1)[: high - low], mixb[GP : 2 * GP, :])
-        for c in range(ROWS // 128):
-            cols = slice(c * 128, (c + 1) * 128)
-            resid[low:high, cols] = (
-                resid[low:high, cols].astype(F32) + gains[low:high, 256:384] * total[:, cols]
-            ).astype(BF)
-        store(i).start()
+    for half in range(2):
+        far(1, half).wait_recv()
+        now = slice(half * 256, (half + 1) * 256)
+        for i in range(4):
+            low, high = i * 2 * PART, min((i + 1) * 2 * PART, D)
+            total = acc[low:high, now] + exact(
+                weights(i, 1, 1)[: high - low], mixb[GP : 2 * GP, now]
+            )
+            for c in range(2):
+                cols = slice(half * 256 + c * 128, half * 256 + (c + 1) * 128)
+                resid[low:high, cols] = (
+                    resid[low:high, cols].astype(F32)
+                    + gains[low:high, 256:384] * total[:, c * 128 : (c + 1) * 128]
+                ).astype(BF)
+            store(i, half).start()
 
     for p in (1, 2, 3):
         to_twin(p).wait_send()
-        swap(p).wait_send()
+        if p > 1:
+            swap(p).wait_send()
         scan_y(p).wait_send()
         scan_z(p).wait_send()
     for second in (0, 1):
@@ -537,7 +550,9 @@
             if p > 1:
                 x_gather(p, second).wait_send()
         x_forward(second).wait_send()
-    swap_onward().wait_send()
+    for half in range(2):
+        for leg in range(2):
+            far(leg, half).wait_send()
     scan_core().wait_send()
     scan_end().wait_send()
 
@@ -549,8 +564,9 @@
     def _():
         halo_right().wait_send()
 
-    for i in range(4):
-        store(i).wait()
+    for half in range(2):
+        for i in range(4):
+            store(i, half).wait()
 
 
 def body(
@@ -591,7 +607,7 @@
             pltpu.VMEM((NBR, TT, 128), F32),
             pltpu.VMEM((FR, NBR, ROWS), F32),
             pltpu.VMEM(((2 * WIN + 1) * 128, 128), BF),
-            pltpu.SemaphoreType.DMA((13,)),
+            pltpu.SemaphoreType.DMA((17,)),
             pltpu.SemaphoreType.DMA((MESSAGES,)),
             pltpu.SemaphoreType.DMA((MESSAGES,)),
         ],

time: 86.2 us -> 85.9 us (level)
  no operation moved by 1% of the time
where the time goes in v7:
time: 85.9 us; the launch traced here: 85.5 us
  Pallas kernels  82.3 us (96%)
  local copies, waits for them, and re-layouts  3.18 us (4%)
    pallas_call x1, Pallas kernels, body(): pl.pallas_call(kernel, out_shape=jax.ShapeDtypeStruct((D, ROWS), BF), in_...  82.3 us
    unnamed x1, local copies, waits for them, and re-layouts  3.18 us

profile of v7, /device:TPU:0, one launch (start us, length us, event | category | flops | bytes accessed | tf_op | source)
XLA Modules:
  0.0 85.5 jit_solution(15284384075495622514)
XLA Ops:
  0.0 82.3 %shard_map.118 = bf16[2240,512]{1,0:T(8,128)(2,1)} custom-call(bf16[2240,2048]{1,0:T(8,128)(2,1)} %bitcast.9, f32[2240]{0:T(1024)} %scale_ref.1, f32[2240]{0:T(1024)} %shift_ref.1, f32[2240]{0:T(1024)} %gate_ref.1, bf16[560,2240]{1,0:T(8,128)(2,1)} %bitcast.11, bf16[560,2240]{1,0:T(8,128)(2,1)} %bitcast.12, bf16[560,2240]{1,0:T(8,128)(2,1)} %bitcast.13, ...), custom_call_target="tpu_custom_call" | custom-call | tf_op jit(solution)/shard_map/pallas_call | solution.py:579
  82.3 3.2 %copy.14 = bf16[512,2240]{0,1:T(8,128)(2,1)} copy(bf16[512,2240]{0,1:T(8,128)(2,1)} %bitcast.10) | data formatting | bytes 4587520

commit v8 on v7

--- a/solution.py
+++ b/solution.py
@@ -185,25 +185,22 @@
     )
 
     def norm(f):
-        rows = 32
-
         def squares(i, total):
-            x = tok[f, pl.ds(pl.multiple_of(i * rows, rows), rows), :].astype(F32)
-            return total + jnp.sum((x * x).reshape(rows // 8, 8, ROWS), axis=0)
-
-        total = lax.fori_loop(0, D // rows, squares, jnp.zeros((8, ROWS), F32), unroll=2)
+            x = tok[f, pl.ds(pl.multiple_of(i * 112, 112), 112), :].astype(F32)
+            return total + jnp.sum((x * x).reshape(112 // 8, 8, ROWS), axis=0)
+
+        total = lax.fori_loop(0, D // 112, squares, jnp.zeros((8, ROWS), F32))
         inverse = lax.rsqrt(jnp.sum(total, axis=0, keepdims=True) * (1.0 / D) + EPS)
 
         def scale(i, _):
-            r = pl.ds(pl.multiple_of(i * rows, rows), rows)
-            gain, shift = gains[r, 0:128], gains[r, 128:256]
-            for c in range(ROWS // 128):
-                cols = slice(c * 128, (c + 1) * 128)
-                x = tok[f, r, cols].astype(F32)
-                tok[f, r, cols] = (x * inverse[:, cols] * gain + shift).astype(BF)
+            r = pl.ds(pl.multiple_of(i * 64, 64), 64)
+            gain = jnp.concatenate([gains[r, 0:128]] * (ROWS // 128), axis=1)
+            shift = jnp.concatenate([gains[r, 128:256]] * (ROWS // 128), axis=1)
+            x = tok[f, r, :].astype(F32)
+            tok[f, r, :] = (x * inverse * gain + shift).astype(BF)
             return 0
 
-        lax.fori_loop(0, D // rows, scale, 0, unroll=2)
+        lax.fori_loop(0, D // 64, scale, 0)
 
     def halo_left():
         return remote(HALO, vbuf.at[pl.ds(2, 2)], vbuf.at[pl.ds(6, 2)], left)
@@ -264,7 +261,7 @@
             scur[h, 0:HD, :] = state
             sloc[f, h] = state
 
-        @pl.when(f == 3)
+        @pl.when(f == 2)
         def _():
             x_arrived(1)
 
@@ -379,7 +376,6 @@
             rel[f, n : n + 1, :] = listed[f : f + 1]
 
     query(3)
-    query(0)
 
     for step in (1, 2, 3):
         scan_y(step).wait_recv()
@@ -424,7 +420,6 @@
 
     window(1)
     window(2)
-    window(3)
 
     for step in (1, 2, 3):
         scan_z(step).wait_recv()
@@ -442,7 +437,7 @@
         side_pass(p, 1).wait_recv()
         to_twin(p).start()
 
-    window(0)
+    window(3)
 
     scan_end().wait_recv()
     for h in range(NH):
@@ -491,8 +486,10 @@
     for p in (2, 3):
         attend(p)
         swap(p).start()
+    query(0)
     far(0, 0).wait_recv()
     far(1, 0).start()
+    window(0)
     attend(0)
     far(0, 1).wait_recv()
     far(1, 1).start()

time: 85.9 us -> 84.9 us (0.988)
  Pallas kernels: 82.3 us -> 81.2 us
    pallas_call x1, Pallas kernels: 82.3 us -> 81.2 us  [body(): pl.pallas_call(kernel, out_shape=jax.ShapeDtypeStruct((D, ROWS), BF), in_...]
where the time goes in v8:
time: 84.9 us; the launch traced here: 84.4 us
  Pallas kernels  81.2 us (96%)
  local copies, waits for them, and re-layouts  3.18 us (4%)
    pallas_call x1, Pallas kernels, body(): pl.pallas_call(kernel, out_shape=jax.ShapeDtypeStruct((D, ROWS), BF), in_...  81.2 us
    unnamed x1, local copies, waits for them, and re-layouts  3.18 us

profile of v8, /device:TPU:0, one launch (start us, length us, event | category | flops | bytes accessed | tf_op | source)
XLA Modules:
  0.0 84.4 jit_solution(11050727577849915047)
XLA Ops:
  0.0 81.2 %shard_map.118 = bf16[2240,512]{1,0:T(8,128)(2,1)} custom-call(bf16[2240,2048]{1,0:T(8,128)(2,1)} %bitcast.9, f32[2240]{0:T(1024)} %scale_ref.1, f32[2240]{0:T(1024)} %shift_ref.1, f32[2240]{0:T(1024)} %gate_ref.1, bf16[560,2240]{1,0:T(8,128)(2,1)} %bitcast.11, bf16[560,2240]{1,0:T(8,128)(2,1)} %bitcast.12, bf16[560,2240]{1,0:T(8,128)(2,1)} %bitcast.13, ...), custom_call_target="tpu_custom_call" | custom-call | tf_op jit(solution)/shard_map/pallas_call | solution.py:576
  81.2 3.2 %copy.14 = bf16[512,2240]{0,1:T(8,128)(2,1)} copy(bf16[512,2240]{0,1:T(8,128)(2,1)} %bitcast.10) | data formatting | bytes 4587520
